TPU v7x, 32 devices: a whole 2x2x4 slice. The times are simulated.
32 devices in a mesh: videos: 2 (over x), rows: 16 (over z, y, core).
Axes of the slice: x: 2, y: 2, z: 4, core: 2. Of those that a mesh axis runs over, the one named last changes fastest.
Arguments:
- latents: bfloat16 [4, 32, 64, 384], P('videos', 'rows'), parts along dimension 0, may hold values from -6 to 6
- conv_cache: bfloat16 [4, 32, 64, 384], P('videos', 'rows'), parts along dimension 0, may hold values from -4 to 4
- norm_gain: float32 [384], replicated, may hold values from 0.1 to 1.9
- conv_weight: bfloat16 [3, 3, 3, 384, 384], replicated, may hold values from -0.0625 to 0.0625
- attn_gain: float32 [384], replicated, may hold values from 0.1 to 1.9
- query_weight: bfloat16 [384, 384], replicated, may hold values from -3 to 3
- key_weight: bfloat16 [384, 384], replicated, may hold values from -3 to 3
- value_weight: bfloat16 [384, 384], replicated, may hold values from -0.3125 to 0.3125
- out_weight: bfloat16 [384, 384], replicated, may hold values from -0.3125 to 0.3125
- up_weight: bfloat16 [3, 3, 384, 192], replicated, may hold values from -0.109375 to 0.109375
Outputs:
- decoded: bfloat16 [4, 64, 128, 192], P('videos', 'rows'), parts along dimension 0
- next_cache: bfloat16 [4, 32, 64, 384], P('videos', 'rows'), parts along dimension 0
There are 2 independent parts, one for each index of `videos`. A program takes and returns all parts, laid end to end along the dimension named above; an argument that names none is the same for every part. Nothing has to cross between parts.
All inputs are finite; a program needn't handle non-finite values.
Results may differ from a plain program's by a relative error of at most 0.0058.
Values may be sent and summed in bfloat16 or wider, within the bound.
No kernel may reach another device: no remote copies, remote signals or barrier semaphores. Data moves between devices by JAX's collectives and lax.ppermute only.
A program may use at most 128 MiB of HBM per device.

v0:
```python
import functools

import jax
import jax.numpy as jnp
from jax import lax
from jax.experimental import pallas as pl
from jax.experimental.pallas import tpu as pltpu
from jax.sharding import PartitionSpec as P

BF16 = jnp.bfloat16
F32 = jnp.float32
EPS = 1e-06
MIB = 1024 * 1024
EXTRA = 16


def normalize(values, gain):
    return values * lax.rsqrt(jnp.mean(values * values, axis=-1, keepdims=True) + EPS) * gain


def activate(values, gain):
    normed = normalize(values.astype(F32), gain)
    return (normed / (1.0 + jnp.exp(-normed))).astype(BF16)


def vmem():
    return pl.BlockSpec(memory_space=pltpu.VMEM)


def params(mib):
    return pltpu.CompilerParams(vmem_limit_bytes=mib * MIB)


def cost(flops, size, exps=0):
    return pl.CostEstimate(flops=flops, bytes_accessed=size, transcendentals=exps)


def edges_kernel(latents_ref, cache_ref, edge_ref, both_ref, sems):
    core = lax.axis_index("rows") % 2
    row = core * (latents_ref.shape[1] - 1)
    copies = [
        pltpu.make_async_copy(cache_ref.at[:, row], edge_ref.at[pl.ds(0, 2)], sems.at[0]),
        pltpu.make_async_copy(latents_ref.at[:, row], edge_ref.at[pl.ds(2, 2)], sems.at[1]),
        pltpu.make_async_copy(cache_ref.at[1], both_ref.at[core], sems.at[2]),
        pltpu.make_async_copy(latents_ref.at[0], both_ref.at[1 + core], sems.at[3]),
    ]
    for copy in copies:
        copy.start()

    @pl.when(core == 0)
    def _():
        last = pltpu.make_async_copy(latents_ref.at[1], both_ref.at[2], sems.at[4])
        last.start()
        last.wait()

    @pl.when(core == 1)
    def _():
        last = pltpu.make_async_copy(cache_ref.at[0], both_ref.at[0], sems.at[4])
        last.start()
        last.wait()

    for copy in copies:
        copy.wait()


def stage(weight_ref, target, sems, time):
    channels = weight_ref.shape[-1]
    return [
        pltpu.make_async_copy(
            weight_ref.at[time, :, col],
            target.at[:, :, pl.ds(col * channels, channels)],
            sems.at[col],
        )
        for col in range(3)
    ]


def prepare_kernel(
    latents_ref,
    cache_ref,
    weight_ref,
    gain_ref,
    act_ref,
    own_ref,
    base_ref,
    staged_ref,
    latents,
    cache,
    gain,
    sems,
    weight_sems,
):
    channels = latents_ref.shape[-1]
    core = lax.axis_index("rows") % 2
    loads = [
        pltpu.make_async_copy(latents_ref, latents, sems.at[0]),
        pltpu.make_async_copy(cache_ref, cache, sems.at[1]),
        pltpu.make_async_copy(gain_ref, gain, sems.at[2]),
    ]
    copies = [
        copy
        for time in range(2)
        for copy in stage(weight_ref, staged_ref.at[time], weight_sems.at[time], time)
    ]
    for copy in loads + copies:
        copy.start()
    for copy in loads:
        copy.wait()
    act_ref[...] = activate(latents[...], gain[...].reshape(1, channels))
    base_ref[...] = latents[core]
    own_ref[0] = cache[core]
    own_ref[2] = act_ref[core]

    @pl.when(core == 0)
    def _():
        own_ref[1] = cache[1]

    @pl.when(core == 1)
    def _():
        own_ref[1] = act_ref[0]

    for copy in copies:
        copy.wait()


def conv_kernel(
    width,
    own_ref,
    base_ref,
    swap_ref,
    edge_ref,
    far_ref,
    norm_gain_ref,
    attn_gain_ref,
    staged_ref,
    weight_ref,
    front_ref,
    back_ref,
    resid_ref,
    held,
    base,
    total,
    last_weights,
    sems,
):
    channels = own_ref.shape[-1]
    core = lax.axis_index("rows") % 2
    copies = stage(weight_ref, last_weights, sems, 2)
    for copy in copies:
        copy.start()
    own = 2 * width
    mine = pl.multiple_of((1 + 2 * core) * width, width)
    other = pl.multiple_of((3 - 2 * core) * width, width)
    near = pl.multiple_of(5 * core * width, width)
    far = pl.multiple_of(5 * (1 - core) * width, width)
    gain = norm_gain_ref[...].reshape(1, channels)

    def place(time, convert):
        held[time, pl.ds(mine, own), :] = own_ref[time]
        held[time, pl.ds(other, own), :] = convert(swap_ref[time])
        held[time, pl.ds(near, width), :] = convert(edge_ref[time + core])
        held[time, pl.ds(far, width), :] = convert(far_ref[time + core])

    place(0, lambda v: v)

    @pl.when(core == 0)
    def _():
        place(1, lambda v: v)

    @pl.when(core == 1)
    def _():
        place(1, lambda v: activate(v, gain))

    place(2, lambda v: activate(v, gain))
    base[pl.ds(pl.multiple_of(2 * core * width, width), own), :] = base_ref[...].astype(F32)
    base[pl.ds(pl.multiple_of(2 * (1 - core) * width, width), own), :] = swap_ref[2].astype(F32)

    span = 4 * width
    for time in range(3):
        lhs = jnp.concatenate(
            [held[time, row * width : row * width + span, :] for row in range(3)], axis=1
        )
        if time == 2:
            for copy in copies:
                copy.wait()
        rhs = staged_ref[time] if time < 2 else last_weights[...]
        rhs = rhs.reshape(3 * channels, 3 * channels)
        part = jnp.dot(lhs, rhs, preferred_element_type=F32)
        if time == 0:
            total[...] = part
        else:
            total[...] += part
    column = lax.broadcasted_iota(jnp.int32, (span, 1), 0) % width
    left = pltpu.roll(total[:, :channels], 1, axis=0)
    right = pltpu.roll(total[:, 2 * channels :], span - 1, axis=0)
    conv_out = total[:, channels : 2 * channels]
    conv_out = conv_out + jnp.where(column == 0, 0.0, left)
    conv_out = conv_out + jnp.where(column == width - 1, 0.0, right)
    resid = base[...] + conv_out
    resid_ref[...] = resid
    size = jnp.mean(resid * resid, axis=-1, keepdims=True) + EPS
    normed = resid * lax.rsqrt(size) * attn_gain_ref[...].reshape(1, channels)
    edges = jnp.sqrt(jnp.concatenate([size[:width], size[span - width :]], axis=0))
    across = jnp.transpose(jnp.broadcast_to(edges, (2 * width, 128)))[:EXTRA]
    high = across.astype(BF16).astype(F32)
    line = lax.broadcasted_iota(jnp.int32, (EXTRA, 1), 0)
    extra = jnp.where(line == 0, high, jnp.where(line == 1, across - high, 0.0)).astype(BF16)
    half = span // 2
    for ref, low in ((front_ref, 0), (back_ref, half)):
        ref[:half] = normed[low : low + half].astype(BF16)
        ref[half:] = jnp.zeros((EXTRA, channels), BF16)
        ref[half:, : 2 * width] = extra


def nt_dot(a, b):
    return lax.dot_general(a, b, (((1,), (1,)), ((), ())), preferred_element_type=F32)


def lead(scale, normed, query_ref, key_ref):
    queries = jnp.dot(normed, query_ref[...], preferred_element_type=F32).astype(BF16)
    return (nt_dot(queries, key_ref[...]) * scale).astype(BF16)


def whole(pair):
    return jnp.concatenate([half[: half.shape[0] - EXTRA] for half in pair], axis=0)


def pairs_of(refs):
    return [(refs[i], refs[i + 1]) for i in range(0, len(refs), 2)]


def fold(values, combine, total):
    for lane in range(0, values.shape[1], 128):
        piece = values[:, lane : lane + 128]
        total = piece if total is None else combine(total, piece)
    return total


def attend(queries, keys, scores, start, peak, sums, added):
    height = queries.shape[0]
    top = None
    for i, key in enumerate(keys):
        part = nt_dot(queries, key)
        scores[i, start : start + height] = part
        top = fold(part, jnp.maximum, top)
    top = jnp.max(top, axis=-1, keepdims=True)
    if peak is not None:
        top = jnp.maximum(top, peak)
        shrink = jnp.exp2(peak - top)
        sums = sums * shrink
        added = added * shrink
    for i, key in enumerate(keys):
        weights = jnp.exp2(scores[i, start : start + height] - top)
        sums = fold(weights, jnp.add, sums)
        part = jnp.dot(weights.astype(BF16), key, preferred_element_type=F32)
        added = part if added is None else added + part
    return top, sums, added


def early_kernel(scale, query_ref, key_ref, *refs):
    blocks = pairs_of(refs[:-5])
    own_query_ref, peak_ref, sums_ref, added_ref, scores = refs[-5:]
    keys = [whole(pair) for pair in blocks]
    queries = lead(scale, keys[0], query_ref, key_ref)
    own_query_ref[...] = queries
    peak, sums, added = attend(queries, keys, scores, 0, None, None, None)
    peak_ref[...] = jnp.broadcast_to(peak, peak_ref.shape)
    sums_ref[...] = sums
    added_ref[...] = added


def late_kernel(
    width,
    scale,
    sources,
    early,
    own_query_ref,
    peak_ref,
    sums_ref,
    added_ref,
    resid_ref,
    gain_ref,
    query_ref,
    key_ref,
    value_ref,
    out_weight_ref,
    *refs,
):
    count = len(sources)
    blocks = pairs_of(refs[: 2 * count])
    mid_ref, swap_ref, scores, mid, halo, sizes = refs[2 * count :]
    place = lax.axis_index("rows")
    core = place % 2
    chip = place // 2
    own, channels = own_query_ref.shape
    half = own // 2
    chips = len(sources[0])

    for block, origin in zip(blocks, sources):
        for step, part, first, low in (
            (-1, block[1], half - width, 0),
            (1, block[0], 0, width),
        ):
            takers = [k for k in range(chips) if origin[k] == k + step]
            if not takers:
                continue
            wanted = chip == takers[0]
            for k in takers[1:]:
                wanted = jnp.logical_or(wanted, chip == k)

            @pl.when(wanted)
            def _(part=part, first=first, low=low):
                halo[low : low + width] = part[first : first + width, :]
                sizes[low // width] = part[half : half + EXTRA, : 2 * width]

    no_above = chip == 0
    no_below = chip == chips - 1

    @pl.when(no_above)
    def _():
        halo[:width] = jnp.zeros((width, channels), BF16)
        sizes[0] = jnp.zeros((EXTRA, 2 * width), BF16)

    @pl.when(no_below)
    def _():
        halo[width:] = jnp.zeros((width, channels), BF16)
        sizes[1] = jnp.zeros((EXTRA, 2 * width), BF16)

    def column(index):
        parts = sizes[index].astype(F32)
        line = parts[0:1] + parts[1:2]
        return jnp.transpose(jnp.broadcast_to(line, (128, 2 * width)))[:, :1]

    edge_rows = halo[...]
    edge_size = jnp.concatenate([column(0)[width:], column(1)[:width]], axis=0)
    edge_resid = edge_rows.astype(F32) * edge_size / gain_ref[...].reshape(1, channels)
    edge_query = lead(scale, edge_rows, query_ref, key_ref)
    keys = [whole(pair) for pair in blocks]
    _, edge_sums, edge_added = attend(edge_query, keys, scores, own, None, None, None)
    _, own_sums, own_added = attend(
        own_query_ref[...],
        keys[early:],
        scores,
        0,
        peak_ref[:, :1],
        sums_ref[...],
        added_ref[...],
    )

    def finish(added, sums):
        return (added / jnp.sum(sums, axis=-1, keepdims=True)).astype(BF16)

    mixed = jnp.concatenate([finish(own_added, own_sums), finish(edge_added, edge_sums)], axis=0)
    attended = jnp.dot(mixed, value_ref[...], preferred_element_type=F32).astype(BF16)
    projected = jnp.dot(attended, out_weight_ref[...], preferred_element_type=F32)
    inner = own + width
    mid[width:inner] = (resid_ref[...] + projected[:own]).astype(BF16)
    edges = edge_resid + projected[own:]
    mid[:width] = jnp.where(no_above, 0.0, edges[:width]).astype(BF16)
    mid[inner:] = jnp.where(no_below, 0.0, edges[width:]).astype(BF16)
    mid_ref[...] = mid[pl.ds(pl.multiple_of(2 * core * width, width), 4 * width), :]
    swap_ref[...] = mid[pl.ds(pl.multiple_of(2 * (1 - core) * width, width), 4 * width), :]


def up_kernel(width, own, rows_ref, weight_ref, *refs):
    out_ref, fine, total, result_ref, sem = refs[-5:]
    core = lax.axis_index("rows") % 2
    frame = core if own else 1 - core
    channels = rows_ref.shape[1]
    outputs = weight_ref.shape[2]
    wide = 2 * width
    lane = lax.broadcasted_iota(jnp.int32, (1, wide), 1)
    lhs = weight_ref[...].reshape(9 * outputs, channels)
    values = rows_ref[...].astype(F32)
    pieces = []
    for i in range(channels // 128):
        piece = values[:, 128 * i : 128 * (i + 1)]
        fine[i, pl.ds(0, 4 * width, stride=2), :] = piece
        fine[i, pl.ds(1, 4 * width, stride=2), :] = piece
        pieces.append(fine[i].astype(BF16))
    total[...] = nt_dot(lhs, jnp.concatenate(pieces, axis=1))
    for row in range(4):
        low = row // 2 + 1
        picks = (low - 1, low, low) if row % 2 == 0 else (low, low, low + 1)
        taps = []
        for col in range(3):
            tap = None
            for j, pick in enumerate(picks):
                piece = total[
                    (3 * j + col) * outputs : (3 * j + col + 1) * outputs,
                    pick * wide : (pick + 1) * wide,
                ]
                tap = piece if tap is None else tap + piece
            taps.append(tap)
        result = taps[1]
        result = result + jnp.where(lane == 0, 0.0, pltpu.roll(taps[0], 1, axis=1))
        result = result + jnp.where(lane == wide - 1, 0.0, pltpu.roll(taps[2], wide - 1, axis=1))
        result_ref[row] = result.astype(BF16)
    copy = pltpu.make_async_copy(result_ref, out_ref.at[frame], sem)
    copy.start()
    copy.wait()


def gather_blocks(halves, count):
    chips = count // 2
    depth = 2 if chips % 2 == 0 else 1
    length = chips // depth

    ring = [0] + list(range(1, length, 2)) + list(range(2, length, 2))[::-1]
    follow = {a: ring[(i + 1) % length] for i, a in enumerate(ring)}
    onward = {a * depth + b: follow[a] * depth + b for a in range(length) for b in range(depth)}
    backward = {target: source for source, target in onward.items()}
    across = {k: k ^ 1 for k in range(chips)}

    def send(values, targets):
        pairs = [(2 * k + c, 2 * targets[k] + c) for k in range(chips) for c in range(2)]
        return lax.ppermute(values, "rows", pairs)

    def moved(origin, targets):
        return {targets[k]: origin[k] for k in range(chips)}

    here = {k: k for k in range(chips)}
    blocks = [list(halves)]
    origins = [here]
    crossed, crossed_origins = [], []
    back = []
    if length > 1:
        back = [send(values, backward) for values in halves]
    if depth == 2:
        crossed.append([send(values, across) for values in halves])
        crossed_origins.append(moved(here, across))
    waits = {(1, 1): [(back, 0)], (2, 0): [(back, 1)]}
    far = []
    for step in range(1, length - 1):
        blocks.append([send(values, onward) for values in blocks[-1]])
        origins.append(moved(origins[-1], onward))
        if depth == 2 and step == 1:
            far = [send(values, backward) for values in crossed[0]]
            waits[(2, 1)] = [(far, 0)]
        for h in range(2):
            tied = [(blocks[-1], h)]
            if depth == 2:
                tied.append((crossed[-1], h))
            tied = tied + waits.get((step, h), [])
            fixed = lax.optimization_barrier(tuple(where[i] for where, i in tied))
            for (where, i), value in zip(tied, fixed):
                where[i] = value
        if depth == 2:
            crossed.append([send(values, across) for values in blocks[-1]])
            crossed_origins.append(moved(origins[-1], across))
    if depth == 2 and length > 1 and not far:
        far = [send(values, backward) for values in crossed[0]]
    if back:
        blocks.append(back)
        origins.append(moved(here, backward))
    late, late_origins = [], []
    if crossed:
        late, late_origins = [crossed.pop()], [crossed_origins.pop()]
    if far:
        late.append(far)
        late_origins.append(moved(moved(here, across), backward))
    return blocks + crossed, origins + crossed_origins, late, late_origins


def shards(
    latents,
    conv_cache,
    norm_gain,
    conv_weight,
    attn_gain,
    query_weight,
    key_weight,
    value_weight,
    out_weight,
    up_weight,
):
    frames, rows_here, width, channels = latents.shape
    outputs = up_weight.shape[3]
    count = lax.axis_size("rows")
    span = 2 * rows_here * width
    own = rows_here * width
    edge = jax.ShapeDtypeStruct((width, channels), BF16)
    anywhere = pl.BlockSpec(memory_space=pl.ANY)
    hbm = pl.BlockSpec(memory_space=pltpu.HBM)

    chips = count // 2
    swap = [(2 * k + c, 2 * k + 1 - c) for k in range(chips) for c in range(2)]
    neighbour = [(2 * k + 1, 2 * k + 2) for k in range(chips - 1)]
    neighbour = neighbour + [(target, source) for source, target in neighbour]

    latents_in = pltpu.with_memory_space_constraint(latents, pltpu.HBM)
    cache_in = pltpu.with_memory_space_constraint(conv_cache, pltpu.HBM)
    edge_rows, both = pl.pallas_call(
        edges_kernel,
        out_shape=(
            jax.ShapeDtypeStruct((2 * frames, width, channels), BF16),
            jax.ShapeDtypeStruct((3, rows_here, width, channels), BF16),
        ),
        in_specs=[hbm] * 2,
        out_specs=(anywhere,) * 2,
        scratch_shapes=[pltpu.SemaphoreType.DMA((5,))],
        cost_estimate=cost(0, 20 * width * channels),
        compiler_params=params(4),
    )(latents_in, cache_in)
    edge_rows = lax.ppermute(edge_rows, "rows", neighbour)
    both = lax.ppermute(both, "rows", swap)
    act, own_rows, base, staged = pl.pallas_call(
        prepare_kernel,
        out_shape=(
            jax.ShapeDtypeStruct((frames, own, channels), BF16),
            jax.ShapeDtypeStruct((3, own, channels), BF16),
            jax.ShapeDtypeStruct((own, channels), BF16),
            jax.ShapeDtypeStruct((2, 3, channels, 3 * channels), BF16),
        ),
        in_specs=[hbm] * 4,
        out_specs=(vmem(), vmem(), vmem(), anywhere),
        scratch_shapes=[
            pltpu.VMEM((frames, own, channels), BF16),
            pltpu.VMEM((frames, own, channels), BF16),
            pltpu.VMEM((channels,), F32),
            pltpu.SemaphoreType.DMA((3,)),
            pltpu.SemaphoreType.DMA((2, 3)),
        ],
        cost_estimate=cost(10 * frames * own * channels, 2 * 27 * channels * channels),
        compiler_params=params(8),
    )(
        pltpu.with_memory_space_constraint(latents.reshape(frames, own, channels), pltpu.HBM),
        pltpu.with_memory_space_constraint(conv_cache.reshape(frames, own, channels), pltpu.HBM),
        pltpu.with_memory_space_constraint(conv_weight, pltpu.HBM),
        pltpu.with_memory_space_constraint(norm_gain, pltpu.HBM),
    )

    edge_rows, base = lax.optimization_barrier((edge_rows, base))
    far_rows = lax.ppermute(edge_rows, "rows", swap)
    half = jax.ShapeDtypeStruct((span // 2 + EXTRA, channels), BF16)
    front, back, resid = pl.pallas_call(
        functools.partial(conv_kernel, width),
        out_shape=(half, half, jax.ShapeDtypeStruct((span, channels), F32)),
        in_specs=[vmem()] * 8 + [hbm],
        out_specs=(vmem(),) * 3,
        scratch_shapes=[
            pltpu.VMEM((3, 6 * width, channels), BF16),
            pltpu.VMEM((span, channels), F32),
            pltpu.VMEM((span, 3 * channels), F32),
            pltpu.VMEM((3, channels, 3 * channels), BF16),
            pltpu.SemaphoreType.DMA((3,)),
        ],
        cost_estimate=cost(2 * 27 * span * channels * channels, 2 * 27 * channels * channels),
        compiler_params=params(20),
    )(
        own_rows,
        base,
        both.reshape(3, own, channels),
        edge_rows,
        far_rows,
        norm_gain,
        attn_gain,
        staged,
        pltpu.with_memory_space_constraint(conv_weight, pltpu.HBM),
    )

    early, early_origins, late, late_origins = gather_blocks((front, back), count)
    sources = [[origin[k] for k in range(chips)] for origin in early_origins + late_origins]
    early_parts = [part for block in early for part in block]
    late_parts = [part for block in late for part in block]

    scale = channels ** (-0.5) * 1.4426950408889634
    wide = span + 2 * width
    lanes = jax.ShapeDtypeStruct((span, 128), F32)
    own_query, peak, sums, added = pl.pallas_call(
        functools.partial(early_kernel, scale),
        out_shape=(
            jax.ShapeDtypeStruct((span, channels), BF16),
            lanes,
            lanes,
            jax.ShapeDtypeStruct((span, channels), F32),
        ),
        in_specs=[vmem()] * (2 + len(early_parts)),
        out_specs=(vmem(),) * 4,
        scratch_shapes=[pltpu.VMEM((len(early), span, span), F32)],
        cost_estimate=cost(
            4 * span * span * len(early) * channels,
            2 * span * channels * len(early),
            span * span * len(early),
        ),
        compiler_params=params(24),
    )(query_weight, key_weight, *early_parts)

    mid, swap_rows = pl.pallas_call(
        functools.partial(late_kernel, width, scale, sources, len(early)),
        out_shape=(jax.ShapeDtypeStruct((4 * width, channels), BF16),) * 2,
        in_specs=[vmem()] * (10 + len(early_parts) + len(late_parts)),
        out_specs=(vmem(),) * 2,
        scratch_shapes=[
            pltpu.VMEM((len(sources), wide, span), F32),
            pltpu.VMEM((wide, channels), BF16),
            pltpu.VMEM((2 * width, channels), BF16),
            pltpu.VMEM((2, EXTRA, 2 * width), BF16),
        ],
        cost_estimate=cost(
            2 * wide * span * len(sources) * channels,
            2 * span * channels * len(sources),
            wide * span * len(sources) // 2,
        ),
        compiler_params=params(28),
    )(
        own_query,
        peak,
        sums,
        added,
        resid,
        attn_gain,
        query_weight,
        key_weight,
        value_weight,
        out_weight,
        *early_parts,
        *late_parts,
    )

    swap_rows = lax.ppermute(swap_rows, "rows", swap)

    fine_shape = (2 * rows_here, outputs, 2 * width)
    taps = jnp.transpose(up_weight, (0, 1, 3, 2))

    def up(is_own, *operands):
        return pl.pallas_call(
            functools.partial(up_kernel, width, is_own),
            out_shape=jax.ShapeDtypeStruct((frames, *fine_shape), BF16),
            in_specs=[vmem()] * 2 + [anywhere] * (len(operands) - 2),
            out_specs=anywhere,
            input_output_aliases={} if is_own else {2: 0},
            scratch_shapes=[
                pltpu.VMEM((channels // 128, 8 * width, 128), F32),
                pltpu.VMEM((9 * outputs, 8 * width), F32),
                pltpu.VMEM(fine_shape, BF16),
                pltpu.SemaphoreType.DMA(()),
            ],
            cost_estimate=cost(
                2 * 9 * outputs * channels * 8 * width, 2 * 9 * outputs * channels
            ),
            compiler_params=params(16),
        )(*operands)

    decoded = up(False, swap_rows, taps, up(True, mid, taps))
    decoded = jnp.transpose(decoded, (0, 1, 3, 2))
    return (decoded, act.reshape(frames, rows_here, width, channels))


def solution(mesh):
    return jax.shard_map(
        shards,
        mesh=mesh,
        in_specs=(
            P("videos", "rows", None, None),
            P("videos", "rows", None, None),
            P(),
            P(),
            P(),
            P(),
            P(),
            P(),
            P(),
            P(),
        ),
        out_specs=(P("videos", "rows", None, None), P("videos", "rows", None, None)),
        check_vma=False,
    )
```

profile of v0, /device:TPU:1, one launch (start us, length us, event | category | flops | bytes accessed | tf_op | source)
XLA Modules:
  0.0 53.5 jit_solution(154834217949367586)
XLA Ops:
  0.7 1.1 %shard_map.114 = (bf16[4,64,384]{2,1,0:T(8,128)(2,1)S(1)}, bf16[3,2,64,384]{3,2,1,0:T(8,128)(2,1)S(1)}) custom-call(bf16[2,2,64,384]{3,2,1,0:T(8,128)(2,1)} %latents_ref.1, bf16[2,2,64,384]{3,2,1,0:T(8,128)(2,1)} %cache_ref.1), custom_call_target="tpu_custom_call" | custom-call | bytes 491520 | tf_op jit(solution)/shard_map/pallas_call | solution.py:493
  1.8 4.5 %collective-permute-start = (bf16[4,64,384]{2,1,0:T(8,128)(2,1)S(1)}, bf16[4,64,384]{2,1,0:T(8,128)(2,1)S(1)}, u32[]{:S(2)}, u32[]{:S(2)}) collective-permute-start(bf16[4,64,384]{2,1,0:T(8,128)(2,1)S(1)} %get-tuple-element.31), channel_id=1, source_target_pairs={{1,2},{3,4},{5,6},{7,8},{9,10},{11,12},{13,14},{2,1},{4,3},{6,5},{... | collective-permute-start | bytes 589832 | tf_op jit(solution)/shard_map/ppermute | solution.py:505
  6.4 3.5 %shard_map.113 = (bf16[2,128,384]{2,1,0:T(8,128)(2,1)}, bf16[3,128,384]{2,1,0:T(8,128)(2,1)S(1)}, bf16[128,384]{1,0:T(8,128)(2,1)S(1)}, bf16[2,3,384,1152]{3,2,1,0:T(8,128)(2,1)S(1)}) custom-call(bf16[2,128,384]{2,1,0:T(8,128)(2,1)} %bitcast.9, bf16[2,128,384]{2,1,0:T(8,128)(2,1)} %bitcast.10, bf16[3,3,3,384,384]{4,3,2,1,0:T(8,128)(2,1)} %weight_ref.3, ...), custom_call_target="tpu_custom_call" | custom-call | flops 983040 | bytes 7962624 | tf_op jit(solution)/shard_map/pallas_call | solution.py:507
  9.9 1.1 %collective-permute-done.edge_ref = bf16[4,64,384]{2,1,0:T(8,128)(2,1)S(1)} collective-permute-done((bf16[4,64,384]{2,1,0:T(8,128)(2,1)S(1)}, bf16[4,64,384]{2,1,0:T(8,128)(2,1)S(1)}, u32[]{:S(2)}, u32[]{:S(2)}) %collective-permute-start) | collective-permute-done | bytes 196640 | tf_op jit(solution)/shard_map/ppermute | solution.py:505
  11.1 1.4 %collective-permute-done.2.far_ref = bf16[4,64,384]{2,1,0:T(8,128)(2,1)S(1)} collective-permute-done((bf16[4,64,384]{2,1,0:T(8,128)(2,1)S(1)}, bf16[4,64,384]{2,1,0:T(8,128)(2,1)S(1)}, u32[]{:S(2)}, u32[]{:S(2)}) %collective-permute-start.2) | collective-permute-done | bytes 196640 | tf_op jit(solution)/shard_map/ppermute | solution.py:534
  12.5 3.6 %shard_map.115 = (bf16[144,384]{1,0:T(8,128)(2,1)S(1)}, bf16[144,384]{1,0:T(8,128)(2,1)S(1)}, f32[256,384]{1,0:T(8,128)S(1)}) custom-call(bf16[3,128,384]{2,1,0:T(8,128)(2,1)S(1)} %get-tuple-element.30.own_ref, bf16[128,384]{1,0:T(8,128)(2,1)S(1)} %get-tuple-element.33.base_ref, bf16[3,128,384]{2,1,0:T(8,128)(2,1)S(1)} %bitcast.6, ...), custom_call_target="tpu_custom_call" | custom-call | flops 2038431744 | bytes 7962624 | tf_op jit(solution)/shard_map/pallas_call | solution.py:536
  16.2 2.3 %collective-permute-start.4 = (bf16[144,384]{1,0:T(8,128)(2,1)S(1)}, bf16[144,384]{1,0:T(8,128)(2,1)S(1)}, u32[]{:S(2)}, u32[]{:S(2)}) collective-permute-start(bf16[144,384]{1,0:T(8,128)(2,1)S(1)} %get-tuple-element.37.refs_0_), channel_id=1, source_target_pairs={{0,2},{1,3},{2,0},{3,1},{4,6},{5,7},{6,4},{7,5},{8,10},{9,11},{10,... | collective-permute-start | bytes 331784 | tf_op jit(solution)/shard_map/ppermute | solution.py:417
  18.4 1.3 %collective-permute-start.3 = (bf16[144,384]{1,0:T(8,128)(2,1)S(1)}, bf16[144,384]{1,0:T(8,128)(2,1)S(1)}, u32[]{:S(2)}, u32[]{:S(2)}) collective-permute-start(bf16[144,384]{1,0:T(8,128)(2,1)S(1)} %get-tuple-element.37.refs_0_), channel_id=1, source_target_pairs={{0,4},{1,5},{2,6},{3,7},{4,12},{5,13},{6,14},{7,15},{8,0},{9,1},{1... | collective-permute-start | bytes 331784 | tf_op jit(solution)/shard_map/ppermute | solution.py:417
  19.7 1.1 %collective-permute-start.7 = (bf16[144,384]{1,0:T(8,128)(2,1)S(1)}, bf16[144,384]{1,0:T(8,128)(2,1)S(1)}, u32[]{:S(2)}, u32[]{:S(2)}) collective-permute-start(bf16[144,384]{1,0:T(8,128)(2,1)S(1)} %get-tuple-element.37.refs_0_), channel_id=1, source_target_pairs={{0,8},{1,9},{2,10},{3,11},{4,0},{5,1},{6,2},{7,3},{8,12},{9,13},{1... | collective-permute-start | bytes 331784 | tf_op jit(solution)/shard_map/ppermute | solution.py:417
  20.9 1.2 %collective-permute-start.5 = (bf16[144,384]{1,0:T(8,128)(2,1)S(1)}, bf16[144,384]{1,0:T(8,128)(2,1)S(1)}, u32[]{:S(2)}, u32[]{:S(2)}) collective-permute-start(bf16[144,384]{1,0:T(8,128)(2,1)S(1)} %get-tuple-element.38.refs_1_), channel_id=1, source_target_pairs={{0,4},{1,5},{2,6},{3,7},{4,12},{5,13},{6,14},{7,15},{8,0},{9,1},{1... | collective-permute-start | bytes 331784 | tf_op jit(solution)/shard_map/ppermute | solution.py:417
  22.1 2.0 %collective-permute-start.10 = (bf16[144,384]{1,0:T(8,128)(2,1)S(1)}, bf16[144,384]{1,0:T(8,128)(2,1)S(1)}, u32[]{:S(2)}, u32[]{:S(2)}) collective-permute-start(bf16[144,384]{1,0:T(8,128)(2,1)S(1)} %get-tuple-element.38.refs_1_), channel_id=1, source_target_pairs={{0,8},{1,9},{2,10},{3,11},{4,0},{5,1},{6,2},{7,3},{8,12},{9,13},{1... | collective-permute-start | bytes 331784 | tf_op jit(solution)/shard_map/ppermute | solution.py:417
  24.1 1.2 %collective-permute-start.9 = (bf16[144,384]{1,0:T(8,128)(2,1)S(1)}, bf16[144,384]{1,0:T(8,128)(2,1)S(1)}, u32[]{:S(2)}, u32[]{:S(2)}) collective-permute-start(bf16[144,384]{1,0:T(8,128)(2,1)S(1)} %collective-permute-done.3.refs_2_), channel_id=1, source_target_pairs={{0,2},{1,3},{2,0},{3,1},{4,6},{5,7},{6,4},{7,5},{8,10},{9,11},{10,... | collective-permute-start | bytes 331784 | tf_op jit(solution)/shard_map/ppermute | solution.py:417
  25.3 3.2 %collective-permute-done.7.refs_6_ = bf16[144,384]{1,0:T(8,128)(2,1)S(1)} collective-permute-done((bf16[144,384]{1,0:T(8,128)(2,1)S(1)}, bf16[144,384]{1,0:T(8,128)(2,1)S(1)}, u32[]{:S(2)}, u32[]{:S(2)}) %collective-permute-start.7) | collective-permute-done | bytes 110624 | tf_op jit(solution)/shard_map/ppermute | solution.py:417
  28.5 2.3 %collective-permute-start.12 = (bf16[144,384]{1,0:T(8,128)(2,1)S(1)}, bf16[144,384]{1,0:T(8,128)(2,1)S(1)}, u32[]{:S(2)}, u32[]{:S(2)}) collective-permute-start(bf16[144,384]{1,0:T(8,128)(2,1)S(1)} %collective-permute-done.5.refs_3_), channel_id=1, source_target_pairs={{0,2},{1,3},{2,0},{3,1},{4,6},{5,7},{6,4},{7,5},{8,10},{9,11},{10,... | collective-permute-start | bytes 331784 | tf_op jit(solution)/shard_map/ppermute | solution.py:417
  32.3 2.2 %collective-permute-start.16 = (bf16[144,384]{1,0:T(8,128)(2,1)S(1)}, bf16[144,384]{1,0:T(8,128)(2,1)S(1)}, u32[]{:S(2)}, u32[]{:S(2)}) collective-permute-start(bf16[144,384]{1,0:T(8,128)(2,1)S(1)} %collective-permute-done.6.refs_9_), channel_id=1, source_target_pairs={{0,8},{1,9},{2,10},{3,11},{4,0},{5,1},{6,2},{7,3},{8,12},{9,13},{1... | collective-permute-start | bytes 331784 | tf_op jit(solution)/shard_map/ppermute | solution.py:417
  35.0 1.5 %collective-permute-done.13.refs_14_ = bf16[144,384]{1,0:T(8,128)(2,1)S(1)} collective-permute-done((bf16[144,384]{1,0:T(8,128)(2,1)S(1)}, bf16[144,384]{1,0:T(8,128)(2,1)S(1)}, u32[]{:S(2)}, u32[]{:S(2)}) %collective-permute-start.13) | collective-permute-done | bytes 110624 | tf_op jit(solution)/shard_map/ppermute | solution.py:417
  36.5 1.0 %collective-permute-done.11.refs_5_ = bf16[144,384]{1,0:T(8,128)(2,1)S(1)} collective-permute-done((bf16[144,384]{1,0:T(8,128)(2,1)S(1)}, bf16[144,384]{1,0:T(8,128)(2,1)S(1)}, u32[]{:S(2)}, u32[]{:S(2)}) %collective-permute-start.11) | collective-permute-done | bytes 110624 | tf_op jit(solution)/shard_map/ppermute | solution.py:417
  37.7 1.6 %shard_map.116 = (bf16[256,384]{1,0:T(8,128)(2,1)S(1)}, f32[256,128]{1,0:T(8,128)S(1)}, f32[256,128]{1,0:T(8,128)S(1)}, f32[256,384]{1,0:T(8,128)S(1)}) custom-call(bf16[384,384]{1,0:T(8,128)(2,1)S(1)} %copy-done, bf16[384,384]{1,0:T(8,128)(2,1)S(1)} %copy-done.1, bf16[144,384]{1,0:T(8,128)(2,1)S(1)} %get-tuple-element.37.refs_0_, ...), custom_call_target="tpu_custom_call" | custom-call | flops 603979776 | bytes 1179648 | tf_op jit(solution)/shard_map/pallas_call | solution.py:570
  39.3 0.9 %collective-permute-done.16.refs_15_ = bf16[144,384]{1,0:T(8,128)(2,1)S(1)} collective-permute-done((bf16[144,384]{1,0:T(8,128)(2,1)S(1)}, bf16[144,384]{1,0:T(8,128)(2,1)S(1)}, u32[]{:S(2)}, u32[]{:S(2)}) %collective-permute-start.16) | collective-permute-done | bytes 110624 | tf_op jit(solution)/shard_map/ppermute | solution.py:417
  40.2 2.3 %collective-permute-done.15.refs_13_ = bf16[144,384]{1,0:T(8,128)(2,1)S(1)} collective-permute-done((bf16[144,384]{1,0:T(8,128)(2,1)S(1)}, bf16[144,384]{1,0:T(8,128)(2,1)S(1)}, u32[]{:S(2)}, u32[]{:S(2)}) %collective-permute-start.15) | collective-permute-done | bytes 110624 | tf_op jit(solution)/shard_map/ppermute | solution.py:417
  42.5 2.7 %shard_map.117 = (bf16[256,384]{1,0:T(8,128)(2,1)S(1)}, bf16[256,384]{1,0:T(8,128)(2,1)S(1)}) custom-call(bf16[256,384]{1,0:T(8,128)(2,1)S(1)} %get-tuple-element.49.own_query_ref, f32[256,128]{1,0:T(8,128)S(1)} %get-tuple-element.50.peak_ref, f32[256,128]{1,0:T(8,128)S(1)} %get-tuple-element.51.sums_ref, f32[256,384]{1,0:T(8,128)S(1)} %get-tuple-element.52.added_ref, ...), custom_call_target="tpu_custom_call" | custom-call | flops 603979776 | bytes 1572864 | tf_op jit(solution)/shard_map/pallas_call | solution.py:589
  45.2 4.3 %collective-permute-start.17 = (bf16[256,384]{1,0:T(8,128)(2,1)S(1)}, bf16[256,384]{1,0:T(8,128)(2,1)S(1)}, u32[]{:S(2)}, u32[]{:S(2)}) collective-permute-start(bf16[256,384]{1,0:T(8,128)(2,1)S(1)} %get-tuple-element.55), channel_id=1, source_target_pairs={{0,1},{1,0},{2,3},{3,2},{4,5},{5,4},{6,7},{7,6},{8,9},{9,8},{10,11... | collective-permute-start | bytes 589832 | tf_op jit(solution)/shard_map/ppermute | solution.py:621
  49.5 2.0 %shard_map.118.refs_0_ = bf16[2,4,192,128]{3,2,1,0:T(8,128)(2,1)} custom-call(bf16[256,384]{1,0:T(8,128)(2,1)S(1)} %get-tuple-element.56.rows_ref, bf16[3,3,192,384]{3,2,1,0:T(8,128)(2,1)S(1)} %bitcast.7), custom_call_target="tpu_custom_call" | custom-call | flops 679477248 | bytes 1327104 | tf_op jit(solution)/shard_map/pallas_call | solution.py:627
  51.5 2.0 %shard_map.119 = bf16[2,4,192,128]{3,2,1,0:T(8,128)(2,1)} custom-call(bf16[256,384]{1,0:T(8,128)(2,1)S(1)} %collective-permute-done.17.rows_ref, bf16[3,3,192,384]{3,2,1,0:T(8,128)(2,1)S(1)} %bitcast.8, bf16[2,4,192,128]{3,2,1,0:T(8,128)(2,1)} %shard_map.118.refs_0_), custom_call_target="tpu_custom_call", output_to_operand_aliasing={{}: (2, {})} | custom-call | flops 679477248 | bytes 1327104 | tf_op jit(solution)/shard_map/pallas_call | solution.py:627
  (33 shorter events, 2.4 us)
Async XLA Ops:
  0.6 11.9 %copy-start.4 = (f32[384]{0:T(512)S(1)}, f32[384]{0:T(512)}, u32[]{:S(2)}) copy-start(f32[384]{0:T(512)} %norm_gain_ref.1) | copy-start | bytes 4612
  1.8 9.2 %collective-permute-start = (bf16[4,64,384]{2,1,0:T(8,128)(2,1)S(1)}, bf16[4,64,384]{2,1,0:T(8,128)(2,1)S(1)}, u32[]{:S(2)}, u32[]{:S(2)}) collective-permute-start(bf16[4,64,384]{2,1,0:T(8,128)(2,1)S(1)} %get-tuple-element.31), channel_id=1, source_target_pairs={{1,2},{3,4},{5,6},{7,8},{9,10},{11,12},{13,14},{2,1},{4,3},{6,5},{... | collective-permute-start | bytes 589832 | tf_op jit(solution)/shard_map/ppermute | solution.py:505
  6.3 4.7 %collective-permute-start.1 = (bf16[3,2,64,384]{3,2,1,0:T(8,128)(2,1)S(1)}, bf16[3,2,64,384]{3,2,1,0:T(8,128)(2,1)S(1)}, u32[]{:S(2)}, u32[]{:S(2)}) collective-permute-start(bf16[3,2,64,384]{3,2,1,0:T(8,128)(2,1)S(1)} %get-tuple-element.34), channel_id=1, source_target_pairs={{0,1},{1,0},{2,3},{3,2},{4,5},{5,4},{6,7},{7,6},{8,9},{9,8},{10,11... | collective-permute-start | bytes 884744 | tf_op jit(solution)/shard_map/ppermute | solution.py:506
  11.0 1.4 %collective-permute-start.2 = (bf16[4,64,384]{2,1,0:T(8,128)(2,1)S(1)}, bf16[4,64,384]{2,1,0:T(8,128)(2,1)S(1)}, u32[]{:S(2)}, u32[]{:S(2)}) collective-permute-start(bf16[4,64,384]{2,1,0:T(8,128)(2,1)S(1)} %collective-permute-done.edge_ref), channel_id=1, source_target_pairs={{0,1},{1,0},{2,3},{3,2},{4,5},{5,4},{6,7},{7,6},{8,9},{9,8},{10,11... | collective-permute-start | bytes 589832 | tf_op jit(solution)/shard_map/ppermute | solution.py:534
  12.5 25.2 %copy-start = (bf16[384,384]{1,0:T(8,128)(2,1)S(1)}, bf16[384,384]{1,0:T(8,128)(2,1)}, u32[]{:S(2)}) copy-start(bf16[384,384]{1,0:T(8,128)(2,1)} %query_ref.3) | copy-start | bytes 884740
  12.5 25.2 %copy-start.1 = (bf16[384,384]{1,0:T(8,128)(2,1)S(1)}, bf16[384,384]{1,0:T(8,128)(2,1)}, u32[]{:S(2)}) copy-start(bf16[384,384]{1,0:T(8,128)(2,1)} %key_ref.3) | copy-start | bytes 884740
  12.5 30.0 %copy-start.2 = (bf16[384,384]{1,0:T(8,128)(2,1)S(1)}, bf16[384,384]{1,0:T(8,128)(2,1)}, u32[]{:S(2)}) copy-start(bf16[384,384]{1,0:T(8,128)(2,1)} %value_ref.1) | copy-start | bytes 884740
  12.5 30.0 %copy-start.3 = (bf16[384,384]{1,0:T(8,128)(2,1)S(1)}, bf16[384,384]{1,0:T(8,128)(2,1)}, u32[]{:S(2)}) copy-start(bf16[384,384]{1,0:T(8,128)(2,1)} %out_weight_ref.1) | copy-start | bytes 884740
  16.2 33.4 %copy-start.6 = (bf16[3,3,384,192]{2,3,1,0:T(8,128)(2,1)S(1)}, bf16[3,3,384,192]{2,3,1,0:T(8,128)(2,1)}, u32[]{:S(2)}) copy-start(bf16[3,3,384,192]{2,3,1,0:T(8,128)(2,1)} %param.19) | copy-start | bytes 3981316
  16.2 5.9 %collective-permute-start.4 = (bf16[144,384]{1,0:T(8,128)(2,1)S(1)}, bf16[144,384]{1,0:T(8,128)(2,1)S(1)}, u32[]{:S(2)}, u32[]{:S(2)}) collective-permute-start(bf16[144,384]{1,0:T(8,128)(2,1)S(1)} %get-tuple-element.37.refs_0_), channel_id=1, source_target_pairs={{0,2},{1,3},{2,0},{3,1},{4,6},{5,7},{6,4},{7,5},{8,10},{9,11},{10,... | collective-permute-start | bytes 331784 | tf_op jit(solution)/shard_map/ppermute | solution.py:417
  18.4 5.6 %collective-permute-start.3 = (bf16[144,384]{1,0:T(8,128)(2,1)S(1)}, bf16[144,384]{1,0:T(8,128)(2,1)S(1)}, u32[]{:S(2)}, u32[]{:S(2)}) collective-permute-start(bf16[144,384]{1,0:T(8,128)(2,1)S(1)} %get-tuple-element.37.refs_0_), channel_id=1, source_target_pairs={{0,4},{1,5},{2,6},{3,7},{4,12},{5,13},{6,14},{7,15},{8,0},{9,1},{1... | collective-permute-start | bytes 331784 | tf_op jit(solution)/shard_map/ppermute | solution.py:417
  19.7 8.7 %collective-permute-start.7 = (bf16[144,384]{1,0:T(8,128)(2,1)S(1)}, bf16[144,384]{1,0:T(8,128)(2,1)S(1)}, u32[]{:S(2)}, u32[]{:S(2)}) collective-permute-start(bf16[144,384]{1,0:T(8,128)(2,1)S(1)} %get-tuple-element.37.refs_0_), channel_id=1, source_target_pairs={{0,8},{1,9},{2,10},{3,11},{4,0},{5,1},{6,2},{7,3},{8,12},{9,13},{1... | collective-permute-start | bytes 331784 | tf_op jit(solution)/shard_map/ppermute | solution.py:417
  20.8 7.7 %collective-permute-start.6 = (bf16[144,384]{1,0:T(8,128)(2,1)S(1)}, bf16[144,384]{1,0:T(8,128)(2,1)S(1)}, u32[]{:S(2)}, u32[]{:S(2)}) collective-permute-start(bf16[144,384]{1,0:T(8,128)(2,1)S(1)} %get-tuple-element.38.refs_1_), channel_id=1, source_target_pairs={{0,2},{1,3},{2,0},{3,1},{4,6},{5,7},{6,4},{7,5},{8,10},{9,11},{10,... | collective-permute-start | bytes 331784 | tf_op jit(solution)/shard_map/ppermute | solution.py:417
  20.9 7.6 %collective-permute-start.5 = (bf16[144,384]{1,0:T(8,128)(2,1)S(1)}, bf16[144,384]{1,0:T(8,128)(2,1)S(1)}, u32[]{:S(2)}, u32[]{:S(2)}) collective-permute-start(bf16[144,384]{1,0:T(8,128)(2,1)S(1)} %get-tuple-element.38.refs_1_), channel_id=1, source_target_pairs={{0,4},{1,5},{2,6},{3,7},{4,12},{5,13},{6,14},{7,15},{8,0},{9,1},{1... | collective-permute-start | bytes 331784 | tf_op jit(solution)/shard_map/ppermute | solution.py:417
  22.1 9.4 %collective-permute-start.10 = (bf16[144,384]{1,0:T(8,128)(2,1)S(1)}, bf16[144,384]{1,0:T(8,128)(2,1)S(1)}, u32[]{:S(2)}, u32[]{:S(2)}) collective-permute-start(bf16[144,384]{1,0:T(8,128)(2,1)S(1)} %get-tuple-element.38.refs_1_), channel_id=1, source_target_pairs={{0,8},{1,9},{2,10},{3,11},{4,0},{5,1},{6,2},{7,3},{8,12},{9,13},{1... | collective-permute-start | bytes 331784 | tf_op jit(solution)/shard_map/ppermute | solution.py:417
  24.1 8.2 %collective-permute-start.9 = (bf16[144,384]{1,0:T(8,128)(2,1)S(1)}, bf16[144,384]{1,0:T(8,128)(2,1)S(1)}, u32[]{:S(2)}, u32[]{:S(2)}) collective-permute-start(bf16[144,384]{1,0:T(8,128)(2,1)S(1)} %collective-permute-done.3.refs_2_), channel_id=1, source_target_pairs={{0,2},{1,3},{2,0},{3,1},{4,6},{5,7},{6,4},{7,5},{8,10},{9,11},{10,... | collective-permute-start | bytes 331784 | tf_op jit(solution)/shard_map/ppermute | solution.py:417
  28.5 6.1 %collective-permute-start.8 = (bf16[144,384]{1,0:T(8,128)(2,1)S(1)}, bf16[144,384]{1,0:T(8,128)(2,1)S(1)}, u32[]{:S(2)}, u32[]{:S(2)}) collective-permute-start(bf16[144,384]{1,0:T(8,128)(2,1)S(1)} %collective-permute-done.3.refs_2_), channel_id=1, source_target_pairs={{0,4},{1,5},{2,6},{3,7},{4,12},{5,13},{6,14},{7,15},{8,0},{9,1},{1... | collective-permute-start | bytes 331784 | tf_op jit(solution)/shard_map/ppermute | solution.py:417
  28.5 8.0 %collective-permute-start.12 = (bf16[144,384]{1,0:T(8,128)(2,1)S(1)}, bf16[144,384]{1,0:T(8,128)(2,1)S(1)}, u32[]{:S(2)}, u32[]{:S(2)}) collective-permute-start(bf16[144,384]{1,0:T(8,128)(2,1)S(1)} %collective-permute-done.5.refs_3_), channel_id=1, source_target_pairs={{0,2},{1,3},{2,0},{3,1},{4,6},{5,7},{6,4},{7,5},{8,10},{9,11},{10,... | collective-permute-start | bytes 331784 | tf_op jit(solution)/shard_map/ppermute | solution.py:417
  30.8 5.7 %collective-permute-start.13 = (bf16[144,384]{1,0:T(8,128)(2,1)S(1)}, bf16[144,384]{1,0:T(8,128)(2,1)S(1)}, u32[]{:S(2)}, u32[]{:S(2)}) collective-permute-start(bf16[144,384]{1,0:T(8,128)(2,1)S(1)} %collective-permute-done.4.refs_8_), channel_id=1, source_target_pairs={{0,8},{1,9},{2,10},{3,11},{4,0},{5,1},{6,2},{7,3},{8,12},{9,13},{1... | collective-permute-start | bytes 331784 | tf_op jit(solution)/shard_map/ppermute | solution.py:417
  31.4 6.1 %collective-permute-start.11 = (bf16[144,384]{1,0:T(8,128)(2,1)S(1)}, bf16[144,384]{1,0:T(8,128)(2,1)S(1)}, u32[]{:S(2)}, u32[]{:S(2)}) collective-permute-start(bf16[144,384]{1,0:T(8,128)(2,1)S(1)} %collective-permute-done.5.refs_3_), channel_id=1, source_target_pairs={{0,4},{1,5},{2,6},{3,7},{4,12},{5,13},{6,14},{7,15},{8,0},{9,1},{1... | collective-permute-start | bytes 331784 | tf_op jit(solution)/shard_map/ppermute | solution.py:417
  32.3 7.9 %collective-permute-start.16 = (bf16[144,384]{1,0:T(8,128)(2,1)S(1)}, bf16[144,384]{1,0:T(8,128)(2,1)S(1)}, u32[]{:S(2)}, u32[]{:S(2)}) collective-permute-start(bf16[144,384]{1,0:T(8,128)(2,1)S(1)} %collective-permute-done.6.refs_9_), channel_id=1, source_target_pairs={{0,8},{1,9},{2,10},{3,11},{4,0},{5,1},{6,2},{7,3},{8,12},{9,13},{1... | collective-permute-start | bytes 331784 | tf_op jit(solution)/shard_map/ppermute | solution.py:417
  34.6 5.6 %collective-permute-start.14 = (bf16[144,384]{1,0:T(8,128)(2,1)S(1)}, bf16[144,384]{1,0:T(8,128)(2,1)S(1)}, u32[]{:S(2)}, u32[]{:S(2)}) collective-permute-start(bf16[144,384]{1,0:T(8,128)(2,1)S(1)} %collective-permute-done.8.refs_4_), channel_id=1, source_target_pairs={{0,2},{1,3},{2,0},{3,1},{4,6},{5,7},{6,4},{7,5},{8,10},{9,11},{10,... | collective-permute-start | bytes 331784 | tf_op jit(solution)/shard_map/ppermute | solution.py:417
  37.5 5.0 %collective-permute-start.15 = (bf16[144,384]{1,0:T(8,128)(2,1)S(1)}, bf16[144,384]{1,0:T(8,128)(2,1)S(1)}, u32[]{:S(2)}, u32[]{:S(2)}) collective-permute-start(bf16[144,384]{1,0:T(8,128)(2,1)S(1)} %collective-permute-done.11.refs_5_), channel_id=1, source_target_pairs={{0,2},{1,3},{2,0},{3,1},{4,6},{5,7},{6,4},{7,5},{8,10},{9,11},{10,... | collective-permute-start | bytes 331784 | tf_op jit(solution)/shard_map/ppermute | solution.py:417
  45.2 6.2 %collective-permute-start.17 = (bf16[256,384]{1,0:T(8,128)(2,1)S(1)}, bf16[256,384]{1,0:T(8,128)(2,1)S(1)}, u32[]{:S(2)}, u32[]{:S(2)}) collective-permute-start(bf16[256,384]{1,0:T(8,128)(2,1)S(1)} %get-tuple-element.55), channel_id=1, source_target_pairs={{0,1},{1,0},{2,3},{3,2},{4,5},{5,4},{6,7},{7,6},{8,9},{9,8},{10,11... | collective-permute-start | bytes 589832 | tf_op jit(solution)/shard_map/ppermute | solution.py:621
  (1 other events, 11.9 us)
where the time goes:
time: 53.6 us; the launch traced here: 53.5 us
  starting transfers between devices  24 us (45%)
  Pallas kernels  16.5 us (31%)
  waiting for transfers between devices  12.1 us (23%)
  between operations  0.76 us (1%)
    ppermute x14, starting transfers between devices, send(): return lax.ppermute(values, 'rows', pairs)  15.1 us
    ppermute x14, waiting for transfers between devices, send(): return lax.ppermute(values, 'rows', pairs)  9.57 us
    ppermute x1, starting transfers between devices, shards(): edge_rows = lax.ppermute(edge_rows, 'rows', neighbour)  4.54 us
    ppermute x1, starting transfers between devices, shards(): swap_rows = lax.ppermute(swap_rows, 'rows', swap)  4.26 us
    pallas_call x2, Pallas kernels, up(): pl.pallas_call(functools.partial(up_kernel, width, is_own), out_shape=jax...  3.92 us
    pallas_call x1, Pallas kernels, shards(): pl.pallas_call(functools.partial(conv_kernel, width), out_shape=(half, ha...  3.61 us
    pallas_call x1, Pallas kernels, shards(): pl.pallas_call(prepare_kernel, out_shape=(jax.ShapeDtypeStruct((frames, o...  3.49 us
    pallas_call x1, Pallas kernels, shards(): pl.pallas_call(functools.partial(late_kernel, width, scale, sources, len(...  2.74 us
  transfers between devices with their start and end apart: 18, of which 9 were waited for; matrix products, arithmetic and copies ran while one was open for 0% of the time, Pallas kernels for 13%

commit v1 on v0

v1 whole, which is shorter than its diff:
```python
import functools

import jax
import jax.numpy as jnp
from jax import lax
from jax.experimental import pallas as pl
from jax.experimental.pallas import tpu as pltpu
from jax.sharding import PartitionSpec as P

BF16 = jnp.bfloat16
F32 = jnp.float32
EPS = 1e-06
MIB = 1024 * 1024
EXTRA = 16
STAGED = 2


def normalize(values, gain):
    return values * lax.rsqrt(jnp.mean(values * values, axis=-1, keepdims=True) + EPS) * gain


def activate(values, gain):
    normed = normalize(values.astype(F32), gain)
    return (normed / (1.0 + jnp.exp(-normed))).astype(BF16)


def params(mib):
    return pltpu.CompilerParams(vmem_limit_bytes=mib * MIB)


def cost(flops, size, exps=0):
    return pl.CostEstimate(flops=flops, bytes_accessed=size, transcendentals=exps)


def edges_kernel(latents_ref, cache_ref, edge_ref, both_ref, sems):
    core = lax.axis_index("rows") % 2
    row = core * (latents_ref.shape[1] - 1)
    copies = [
        pltpu.make_async_copy(cache_ref.at[:, row], edge_ref.at[pl.ds(0, 2)], sems.at[0]),
        pltpu.make_async_copy(latents_ref.at[:, row], edge_ref.at[pl.ds(2, 2)], sems.at[1]),
        pltpu.make_async_copy(cache_ref.at[1], both_ref.at[core], sems.at[2]),
        pltpu.make_async_copy(latents_ref.at[0], both_ref.at[1 + core], sems.at[3]),
    ]
    for copy in copies:
        copy.start()

    @pl.when(core == 0)
    def _():
        last = pltpu.make_async_copy(latents_ref.at[1], both_ref.at[2], sems.at[4])
        last.start()
        last.wait()

    @pl.when(core == 1)
    def _():
        last = pltpu.make_async_copy(cache_ref.at[0], both_ref.at[0], sems.at[4])
        last.start()
        last.wait()

    for copy in copies:
        copy.wait()


def start_all(pairs, sems, first=0):
    copies = [
        pltpu.make_async_copy(source, target, sems.at[first + i])
        for i, (source, target) in enumerate(pairs)
    ]
    for copy in copies:
        copy.start()
    return copies


def wait_all(copies):
    for copy in copies:
        copy.wait()


def laid_out(weight_ref, target, time):
    channels = weight_ref.shape[-1]
    return [
        (weight_ref.at[time, :, col], target.at[:, :, pl.ds(col * channels, channels)])
        for col in range(3)
    ]


def activate_kernel(latents_ref, gain_ref, act_ref, latents, gain, act, sems):
    wait_all(start_all([(latents_ref, latents), (gain_ref, gain)], sems))
    act[...] = activate(latents[...], gain[...].reshape(1, latents.shape[-1]))
    wait_all(start_all([(act, act_ref)], sems))


def stage_kernel(latents_ref, cache_ref, weight_ref, own_ref, staged_ref, sems):
    core = lax.axis_index("rows") % 2
    pairs = [(cache_ref.at[core], own_ref.at[0]), (latents_ref.at[core], own_ref.at[2])]
    for time in range(staged_ref.shape[0]):
        pairs = pairs + laid_out(weight_ref, staged_ref.at[time], time)
    copies = start_all(pairs, sems, 1)

    @pl.when(core == 0)
    def _():
        wait_all(start_all([(cache_ref.at[1], own_ref.at[1])], sems))

    @pl.when(core == 1)
    def _():
        wait_all(start_all([(latents_ref.at[0], own_ref.at[1])], sems))

    wait_all(copies)


def conv_kernel(
    width,
    own_ref,
    swap_ref,
    edge_ref,
    far_ref,
    norm_gain_ref,
    attn_gain_ref,
    staged_ref,
    weight_ref,
    front_ref,
    back_ref,
    resid_ref,
    raw,
    second,
    third,
    weights,
    total,
    front,
    back,
    resid,
    norm_gain,
    attn_gain,
    sems,
):
    channels = own_ref.shape[-1]
    core = lax.axis_index("rows") % 2
    own = 2 * width
    span = 4 * width
    staged = staged_ref.shape[0]

    def rows_at(index, count):
        return raw.at[:, pl.ds(pl.multiple_of(index * width, width), count)]

    frames = pl.ds(core, 3)
    small = start_all(
        [
            (own_ref, rows_at(1 + 2 * core, own)),
            (swap_ref, rows_at(3 - 2 * core, own)),
            (edge_ref.at[frames], rows_at(5 * core, width)),
            (far_ref.at[frames], rows_at(5 * (1 - core), width)),
            (norm_gain_ref, norm_gain),
            (attn_gain_ref, attn_gain),
        ],
        sems,
    )
    large = []
    for time in range(3):
        if time < staged:
            pairs = [(staged_ref.at[time], weights.at[time])]
        else:
            pairs = laid_out(weight_ref, weights.at[time], time)
        large.append(start_all(pairs, sems, 6 + 3 * time))
    wait_all(small)
    gain = norm_gain[...].reshape(1, channels)

    def taps(ref, time):
        lhs = jnp.concatenate([ref[row * width : row * width + span] for row in range(3)], axis=1)
        rhs = weights[time].reshape(3 * channels, 3 * channels)
        return jnp.dot(lhs, rhs, preferred_element_type=F32)

    wait_all(large[0])
    total[...] = taps(raw.at[0], 0)
    second[...] = jnp.where(core == 1, activate(raw[1], gain), raw[1])
    third[...] = activate(raw[2], gain)
    wait_all(large[1])
    total[...] += taps(second, 1)
    wait_all(large[2])
    total[...] += taps(third, 2)

    column = lax.broadcasted_iota(jnp.int32, (span, 1), 0) % width
    left = pltpu.roll(total[:, :channels], 1, axis=0)
    right = pltpu.roll(total[:, 2 * channels :], span - 1, axis=0)
    conv_out = total[:, channels : 2 * channels]
    conv_out = conv_out + jnp.where(column == 0, 0.0, left)
    conv_out = conv_out + jnp.where(column == width - 1, 0.0, right)
    value = raw[2, width : width + span].astype(F32) + conv_out
    resid[...] = value
    size = jnp.mean(value * value, axis=-1, keepdims=True) + EPS
    normed = value * lax.rsqrt(size) * attn_gain[...].reshape(1, channels)
    edges = jnp.sqrt(jnp.concatenate([size[:width], size[span - width :]], axis=0))
    across = jnp.transpose(jnp.broadcast_to(edges, (2 * width, 128)))[:EXTRA]
    high = across.astype(BF16).astype(F32)
    line = lax.broadcasted_iota(jnp.int32, (EXTRA, 1), 0)
    extra = jnp.where(line == 0, high, jnp.where(line == 1, across - high, 0.0)).astype(BF16)
    half = span // 2
    for ref, low in ((front, 0), (back, half)):
        ref[:half] = normed[low : low + half].astype(BF16)
        ref[half:] = jnp.zeros((EXTRA, channels), BF16)
        ref[half:, : 2 * width] = extra
    wait_all(start_all([(front, front_ref), (back, back_ref), (resid, resid_ref)], sems))


def nt_dot(a, b):
    return lax.dot_general(a, b, (((1,), (1,)), ((), ())), preferred_element_type=F32)


def lead(scale, normed, query_ref, key_ref):
    queries = jnp.dot(normed, query_ref[...], preferred_element_type=F32).astype(BF16)
    return (nt_dot(queries, key_ref[...]) * scale).astype(BF16)


def pairs_of(refs):
    return [(refs[i], refs[i + 1]) for i in range(0, len(refs), 2)]


def load_keys(blocks, keys, sems, first):
    half = keys.shape[1] // 2
    copies = []
    for i, pair in enumerate(blocks):
        halves = [
            (ref.at[pl.ds(0, half)], keys.at[i, pl.ds(part * half, half)])
            for part, ref in enumerate(pair)
        ]
        copies.append(start_all(halves, sems, first + 2 * i))
    return copies


def fold(values, combine, total):
    for lane in range(0, values.shape[1], 128):
        piece = values[:, lane : lane + 128]
        total = piece if total is None else combine(total, piece)
    return total


def attend(queries, keys, indices, scores, start, peak, sums, added):
    height = queries.shape[0]
    top = None
    for i in indices:
        part = nt_dot(queries, keys[i])
        scores[i, start : start + height] = part
        top = fold(part, jnp.maximum, top)
    top = jnp.max(top, axis=-1, keepdims=True)
    if peak is not None:
        top = jnp.maximum(top, peak)
        shrink = jnp.exp2(peak - top)
        sums = sums * shrink
        added = added * shrink
    for i in indices:
        weights = jnp.exp2(scores[i, start : start + height] - top)
        sums = fold(weights, jnp.add, sums)
        part = jnp.dot(weights.astype(BF16), keys[i], preferred_element_type=F32)
        added = part if added is None else added + part
    return top, sums, added


def early_kernel(scale, count, query_ref, key_ref, *refs):
    blocks = pairs_of(refs[: 2 * count])
    outs, held = refs[2 * count : 2 * count + 4], refs[2 * count + 4 : 2 * count + 8]
    keys, scores, query_weight, key_weight, sems = refs[2 * count + 8 :]
    own_query, peak_out, sums_out, added_out = held
    small = start_all([(query_ref, query_weight), (key_ref, key_weight)], sems)
    loads = load_keys(blocks, keys, sems, 2)
    wait_all(small)
    for copies in loads:
        wait_all(copies)
    queries = lead(scale, keys[0], query_weight, key_weight)
    own_query[...] = queries
    peak, sums, added = attend(queries, keys, range(count), scores, 0, None, None, None)
    peak_out[...] = jnp.broadcast_to(peak, peak_out.shape)
    sums_out[...] = sums
    added_out[...] = added
    wait_all(start_all(list(zip(held, outs)), sems))


def late_kernel(width, scale, above, below, early, count, *refs):
    inputs, refs = refs[:10], refs[10:]
    blocks, refs = pairs_of(refs[: 2 * count]), refs[2 * count :]
    mid_ref, swap_ref = refs[:2]
    held, refs = refs[2:12], refs[12:]
    keys, extras, scores, mid, sems = refs
    own_query, peak, sums, added, resid, gain, query_weight, key_weight, value_weight, out = held
    place = lax.axis_index("rows")
    core = place % 2
    chip = place // 2
    own, channels = own_query.shape
    chips = len(above)

    base = len(held)
    loads = load_keys(blocks, keys, sems, base)
    base = base + 2 * count
    notes = start_all(
        [
            (pair[0].at[pl.ds(own // 2, EXTRA), pl.ds(0, 2 * width)], extras.at[i])
            for i, pair in enumerate(blocks)
        ],
        sems,
        base,
    )
    small = start_all(list(zip(inputs, held)), sems)
    for copies in loads:
        wait_all(copies)
    wait_all(notes)
    wait_all(small)

    def pick(table):
        index = 0
        for k, entry in enumerate(table):
            if entry:
                index = jnp.where(chip == k, entry, index)
        return index

    before, after = pick(above), pick(below)
    no_above = chip == 0
    no_below = chip == chips - 1

    def column(index):
        parts = extras[index].astype(F32)
        line = parts[0:1] + parts[1:2]
        return jnp.transpose(jnp.broadcast_to(line, (128, 2 * width)))[:, :1]

    edge_rows = jnp.concatenate([keys[before][own - width :], keys[after][:width]], axis=0)
    edge_size = jnp.concatenate([column(before)[width:], column(after)[:width]], axis=0)
    edge_resid = edge_rows.astype(F32) * edge_size / gain[...].reshape(1, channels)
    edge_query = lead(scale, edge_rows, query_weight, key_weight)
    _, edge_sums, edge_added = attend(
        edge_query, keys, range(count), scores, own, None, None, None
    )
    _, own_sums, own_added = attend(
        own_query[...],
        keys,
        range(early, count),
        scores,
        0,
        peak[:, :1],
        sums[...],
        added[...],
    )

    def finish(values, parts):
        return (values / jnp.sum(parts, axis=-1, keepdims=True)).astype(BF16)

    mixed = jnp.concatenate([finish(own_added, own_sums), finish(edge_added, edge_sums)], axis=0)
    attended = jnp.dot(mixed, value_weight[...], preferred_element_type=F32).astype(BF16)
    projected = jnp.dot(attended, out[...], preferred_element_type=F32)
    inner = own + width
    mid[width:inner] = (resid[...] + projected[:own]).astype(BF16)
    edges = edge_resid + projected[own:]
    mid[:width] = jnp.where(no_above, 0.0, edges[:width]).astype(BF16)
    mid[inner:] = jnp.where(no_below, 0.0, edges[width:]).astype(BF16)

    def part(index):
        return mid.at[pl.ds(pl.multiple_of(2 * index * width, width), 4 * width)]

    wait_all(start_all([(part(1 - core), swap_ref), (part(core), mid_ref)], sems))


def up_kernel(
    width, mid_ref, swap_ref, weight_ref, out_ref, rows, weights, fine, total, results, sems
):
    core = lax.axis_index("rows") % 2
    channels = mid_ref.shape[1]
    outputs = weight_ref.shape[2]
    wide = 2 * width
    loads = start_all(
        [(mid_ref, rows.at[0]), (weight_ref, weights), (swap_ref, rows.at[1])], sems
    )
    lane = lax.broadcasted_iota(jnp.int32, (1, wide), 1)

    def spread(slot):
        values = rows[slot].astype(F32)
        pieces = []
        for i in range(channels // 128):
            piece = values[:, 128 * i : 128 * (i + 1)]
            fine[slot, i, pl.ds(0, 4 * width, stride=2), :] = piece
            fine[slot, i, pl.ds(1, 4 * width, stride=2), :] = piece
            pieces.append(fine[slot, i].astype(BF16))
        return jnp.concatenate(pieces, axis=1)

    def combine(slot):
        for row in range(4):
            low = row // 2 + 1
            picks = (low - 1, low, low) if row % 2 == 0 else (low, low, low + 1)
            taps = []
            for col in range(3):
                tap = None
                for j, pick in enumerate(picks):
                    piece = total[
                        slot,
                        (3 * j + col) * outputs : (3 * j + col + 1) * outputs,
                        pick * wide : (pick + 1) * wide,
                    ]
                    tap = piece if tap is None else tap + piece
                taps.append(tap)
            result = taps[1]
            result = result + jnp.where(lane == 0, 0.0, pltpu.roll(taps[0], 1, axis=1))
            result = result + jnp.where(
                lane == wide - 1, 0.0, pltpu.roll(taps[2], wide - 1, axis=1)
            )
            results[slot, row] = result.astype(BF16)

    loads[0].wait()
    first = spread(0)
    loads[2].wait()
    second = spread(1)
    loads[1].wait()
    lhs = weights[...].reshape(9 * outputs, channels)
    total[0] = nt_dot(lhs, first)
    total[1] = nt_dot(lhs, second)
    combine(0)
    stores = start_all([(results.at[0], out_ref.at[core])], sems, 3)
    combine(1)
    stores = stores + start_all([(results.at[1], out_ref.at[1 - core])], sems, 4)
    wait_all(stores)


def gather_blocks(halves, count):
    chips = count // 2
    depth = 2 if chips % 2 == 0 else 1
    length = chips // depth

    ring = [0] + list(range(1, length, 2)) + list(range(2, length, 2))[::-1]
    follow = {a: ring[(i + 1) % length] for i, a in enumerate(ring)}
    onward = {a * depth + b: follow[a] * depth + b for a in range(length) for b in range(depth)}
    backward = {target: source for source, target in onward.items()}
    across = {k: k ^ 1 for k in range(chips)}

    def send(values, targets):
        pairs = [(2 * k + c, 2 * targets[k] + c) for k in range(chips) for c in range(2)]
        return lax.ppermute(values, "rows", pairs)

    def moved(origin, targets):
        return {targets[k]: origin[k] for k in range(chips)}

    here = {k: k for k in range(chips)}
    blocks = [list(halves)]
    origins = [here]
    crossed, crossed_origins = [], []
    back = []
    if length > 1:
        back = [send(values, backward) for values in halves]
    if depth == 2:
        crossed.append([send(values, across) for values in halves])
        crossed_origins.append(moved(here, across))
    waits = {(1, 1): [(back, 0)], (2, 0): [(back, 1)]}
    far = []
    for step in range(1, length - 1):
        blocks.append([send(values, onward) for values in blocks[-1]])
        origins.append(moved(origins[-1], onward))
        if depth == 2 and step == 1:
            far = [send(values, backward) for values in crossed[0]]
            waits[(2, 1)] = [(far, 0)]
        for h in range(2):
            tied = [(blocks[-1], h)]
            if depth == 2:
                tied.append((crossed[-1], h))
            tied = tied + waits.get((step, h), [])
            fixed = lax.optimization_barrier(tuple(where[i] for where, i in tied))
            for (where, i), value in zip(tied, fixed):
                where[i] = value
        if depth == 2:
            crossed.append([send(values, across) for values in blocks[-1]])
            crossed_origins.append(moved(origins[-1], across))
    if depth == 2 and length > 1 and not far:
        far = [send(values, backward) for values in crossed[0]]
    if back:
        blocks.append(back)
        origins.append(moved(here, backward))
    late, late_origins = [], []
    if crossed:
        late, late_origins = [crossed.pop()], [crossed_origins.pop()]
    if far:
        late.append(far)
        late_origins.append(moved(moved(here, across), backward))
    return blocks + crossed, origins + crossed_origins, late, late_origins


def shards(
    latents,
    conv_cache,
    norm_gain,
    conv_weight,
    attn_gain,
    query_weight,
    key_weight,
    value_weight,
    out_weight,
    up_weight,
):
    frames, rows_here, width, channels = latents.shape
    outputs = up_weight.shape[3]
    count = lax.axis_size("rows")
    span = 2 * rows_here * width
    own = rows_here * width
    edge = jax.ShapeDtypeStruct((width, channels), BF16)
    anywhere = pl.BlockSpec(memory_space=pl.ANY)
    hbm = pl.BlockSpec(memory_space=pltpu.HBM)

    chips = count // 2
    swap = [(2 * k + c, 2 * k + 1 - c) for k in range(chips) for c in range(2)]
    neighbour = [(2 * k + 1, 2 * k + 2) for k in range(chips - 1)]
    neighbour = neighbour + [(target, source) for source, target in neighbour]

    latents_in = pltpu.with_memory_space_constraint(latents, pltpu.HBM)
    cache_in = pltpu.with_memory_space_constraint(conv_cache, pltpu.HBM)
    edge_rows, both = pl.pallas_call(
        edges_kernel,
        out_shape=(
            jax.ShapeDtypeStruct((2 * frames, width, channels), BF16),
            jax.ShapeDtypeStruct((3, rows_here, width, channels), BF16),
        ),
        in_specs=[hbm] * 2,
        out_specs=(anywhere,) * 2,
        scratch_shapes=[pltpu.SemaphoreType.DMA((5,))],
        cost_estimate=cost(0, 20 * width * channels),
        compiler_params=params(4),
    )(latents_in, cache_in)
    edge_rows = lax.ppermute(edge_rows, "rows", neighbour)
    both = lax.ppermute(both, "rows", swap)
    flat_in = pltpu.with_memory_space_constraint(latents.reshape(frames, own, channels), pltpu.HBM)
    flat_cache = pltpu.with_memory_space_constraint(
        conv_cache.reshape(frames, own, channels), pltpu.HBM
    )
    weight_in = pltpu.with_memory_space_constraint(conv_weight, pltpu.HBM)
    taps_shape = (3, channels, 3 * channels)
    own_rows, staged = pl.pallas_call(
        stage_kernel,
        out_shape=(
            jax.ShapeDtypeStruct((3, own, channels), BF16),
            jax.ShapeDtypeStruct((STAGED, *taps_shape), BF16),
        ),
        in_specs=[hbm] * 3,
        out_specs=(anywhere,) * 2,
        scratch_shapes=[pltpu.SemaphoreType.DMA((3 + 3 * STAGED,))],
        cost_estimate=cost(0, 4 * 9 * STAGED * channels * channels),
        compiler_params=params(4),
    )(flat_in, flat_cache, weight_in)

    edge_rows, own_rows = lax.optimization_barrier((edge_rows, own_rows))
    far_rows = lax.ppermute(edge_rows, "rows", swap)
    half = (span // 2 + EXTRA, channels)
    halo_rows = (6 * width, channels)
    front, back, resid = pl.pallas_call(
        functools.partial(conv_kernel, width),
        out_shape=(
            jax.ShapeDtypeStruct(half, BF16),
            jax.ShapeDtypeStruct(half, BF16),
            jax.ShapeDtypeStruct((span, channels), F32),
        ),
        in_specs=[anywhere] * 7 + [hbm],
        out_specs=(anywhere,) * 3,
        scratch_shapes=[
            pltpu.VMEM((3, *halo_rows), BF16),
            pltpu.VMEM(halo_rows, BF16),
            pltpu.VMEM(halo_rows, BF16),
            pltpu.VMEM((3, *taps_shape), BF16),
            pltpu.VMEM((span, 3 * channels), F32),
            pltpu.VMEM(half, BF16),
            pltpu.VMEM(half, BF16),
            pltpu.VMEM((span, channels), F32),
            pltpu.VMEM((channels,), F32),
            pltpu.VMEM((channels,), F32),
            pltpu.SemaphoreType.DMA((15,)),
        ],
        cost_estimate=cost(2 * 27 * span * channels * channels, 2 * 27 * channels * channels),
        compiler_params=params(24),
    )(
        own_rows,
        both.reshape(3, own, channels),
        edge_rows,
        far_rows,
        norm_gain,
        attn_gain,
        staged,
        weight_in,
    )

    early, early_origins, late, late_origins = gather_blocks((front, back), count)
    sources = early_origins + late_origins
    above, below = (
        [next((i for i, o in enumerate(sources) if o[k] == k + step), 0) for k in range(chips)]
        for step in (-1, 1)
    )
    early_parts = [part for block in early for part in block]
    late_parts = [part for block in late for part in block]

    act = pl.pallas_call(
        activate_kernel,
        out_shape=jax.ShapeDtypeStruct((frames, own, channels), BF16),
        in_specs=[hbm] * 2,
        out_specs=anywhere,
        scratch_shapes=[
            pltpu.VMEM((frames, own, channels), BF16),
            pltpu.VMEM((channels,), F32),
            pltpu.VMEM((frames, own, channels), BF16),
            pltpu.SemaphoreType.DMA((2,)),
        ],
        cost_estimate=cost(20 * frames * own * channels, 4 * frames * own * channels),
        compiler_params=params(8),
    )(flat_in, pltpu.with_memory_space_constraint(norm_gain, pltpu.HBM))

    scale = channels ** (-0.5) * 1.4426950408889634
    wide = span + 2 * width
    square = pltpu.VMEM((channels, channels), BF16)
    state = [((span, channels), BF16), ((span, 128), F32), ((span, 128), F32)]
    state = state + [((span, channels), F32)]
    own_query, peak, sums, added = pl.pallas_call(
        functools.partial(early_kernel, scale, len(early)),
        out_shape=tuple(jax.ShapeDtypeStruct(*item) for item in state),
        in_specs=[anywhere] * (2 + len(early_parts)),
        out_specs=(anywhere,) * 4,
        scratch_shapes=[pltpu.VMEM(*item) for item in state]
        + [
            pltpu.VMEM((len(early), span, channels), BF16),
            pltpu.VMEM((len(early), span, span), F32),
            square,
            square,
            pltpu.SemaphoreType.DMA((max(4, 2 + len(early_parts)),)),
        ],
        cost_estimate=cost(
            4 * span * span * len(early) * channels,
            2 * span * channels * len(early),
            span * span * len(early),
        ),
        compiler_params=params(24),
    )(query_weight, key_weight, *early_parts)

    blocks = len(sources)
    mid, swap_rows = pl.pallas_call(
        functools.partial(late_kernel, width, scale, above, below, len(early), blocks),
        out_shape=(jax.ShapeDtypeStruct((4 * width, channels), BF16),) * 2,
        in_specs=[anywhere] * (10 + 2 * blocks),
        out_specs=(anywhere,) * 2,
        scratch_shapes=[pltpu.VMEM(*item) for item in state]
        + [
            pltpu.VMEM((span, channels), F32),
            pltpu.VMEM((channels,), F32),
            square,
            square,
            square,
            square,
            pltpu.VMEM((blocks, span, channels), BF16),
            pltpu.VMEM((blocks, EXTRA, 2 * width), BF16),
            pltpu.VMEM((blocks, wide, span), F32),
            pltpu.VMEM((wide, channels), BF16),
            pltpu.SemaphoreType.DMA((10 + 3 * blocks,)),
        ],
        cost_estimate=cost(
            2 * wide * span * blocks * channels,
            2 * span * channels * blocks,
            wide * span * blocks // 2,
        ),
        compiler_params=params(36),
    )(
        own_query,
        peak,
        sums,
        added,
        resid,
        attn_gain,
        query_weight,
        key_weight,
        value_weight,
        out_weight,
        *early_parts,
        *late_parts,
    )

    swap_rows = lax.ppermute(swap_rows, "rows", swap)

    fine_shape = (2 * rows_here, outputs, 2 * width)
    decoded = pl.pallas_call(
        functools.partial(up_kernel, width),
        out_shape=jax.ShapeDtypeStruct((frames, *fine_shape), BF16),
        in_specs=[anywhere] * 3,
        out_specs=anywhere,
        scratch_shapes=[
            pltpu.VMEM((2, 4 * width, channels), BF16),
            pltpu.VMEM((3, 3, outputs, channels), BF16),
            pltpu.VMEM((2, channels // 128, 8 * width, 128), F32),
            pltpu.VMEM((2, 9 * outputs, 8 * width), F32),
            pltpu.VMEM((2, *fine_shape), BF16),
            pltpu.SemaphoreType.DMA((5,)),
        ],
        cost_estimate=cost(
            2 * 9 * outputs * channels * 16 * width, 2 * 9 * outputs * channels
        ),
        compiler_params=params(24),
    )(mid, swap_rows, jnp.transpose(up_weight, (0, 1, 3, 2)))
    decoded = jnp.transpose(decoded, (0, 1, 3, 2))
    return (decoded, act.reshape(frames, rows_here, width, channels))


def solution(mesh):
    return jax.shard_map(
        shards,
        mesh=mesh,
        in_specs=(
            P("videos", "rows", None, None),
            P("videos", "rows", None, None),
            P(),
            P(),
            P(),
            P(),
            P(),
            P(),
            P(),
            P(),
        ),
        out_specs=(P("videos", "rows", None, None), P("videos", "rows", None, None)),
        check_vma=False,
    )
```

time: 53.6 us -> 66 us (1.23)
  Pallas kernels: 16.5 us -> 25.5 us
  waiting for transfers between devices: 12.1 us -> 21 us
  starting transfers between devices: 24 us -> 18.5 us
    pallas_call x6, Pallas kernels: 15.4 us -> 24.3 us  [the longest x1 7.07 us: shards(): pl.pallas_call(functools.partial(late_kernel, width, scale, above, below,...]
    ppermute x14, waiting for transfers between devices: 9.57 us -> 17.7 us  [send(): return lax.ppermute(values, 'rows', pairs)]
    ppermute x14, starting transfers between devices: 15.1 us -> 11.2 us  [send(): return lax.ppermute(values, 'rows', pairs)]
    ppermute x1, starting transfers between devices: 4.26 us -> 2.69 us  [shards(): swap_rows = lax.ppermute(swap_rows, 'rows', swap)]
    ppermute x1, waiting for transfers between devices: 1.12 us -> 1.9 us  [shards(): edge_rows = lax.ppermute(edge_rows, 'rows', neighbour)]
  transfers between devices with their start and end apart: 18 -> 18, of which waited for: 9 -> 6; matrix products, arithmetic and copies ran while one was open for 0% -> 0% of each run, Pallas kernels for 13% -> 13%
where the time goes in v1:
time: 66 us; the launch traced here: 65.8 us
  Pallas kernels  25.5 us (39%)
  waiting for transfers between devices  21 us (32%)
  starting transfers between devices  18.5 us (28%)
  between operations  0.83 us (1%)
    ppermute x14, waiting for transfers between devices, send(): return lax.ppermute(values, 'rows', pairs)  17.7 us
    ppermute x14, starting transfers between devices, send(): return lax.ppermute(values, 'rows', pairs)  11.2 us
    pallas_call x1, Pallas kernels, shards(): pl.pallas_call(functools.partial(late_kernel, width, scale, above, below,...  7.07 us
    pallas_call x1, Pallas kernels, shards(): pl.pallas_call(functools.partial(conv_kernel, width), out_shape=(jax.Shap...  4.8 us
    ppermute x1, starting transfers between devices, shards(): edge_rows = lax.ppermute(edge_rows, 'rows', neighbour)  4.54 us
    pallas_call x1, Pallas kernels, shards(): pl.pallas_call(functools.partial(early_kernel, scale, len(early)), out_sh...  4.17 us
    pallas_call x1, Pallas kernels, shards(): pl.pallas_call(functools.partial(up_kernel, width), out_shape=jax.ShapeDt...  3.7 us
    pallas_call x1, Pallas kernels, shards(): pl.pallas_call(stage_kernel, out_shape=(jax.ShapeDtypeStruct((3, own, cha...  2.71 us
  transfers between devices with their start and end apart: 18, of which 6 were waited for; matrix products, arithmetic and copies ran while one was open for 0% of the time, Pallas kernels for 13%

profile of v1, /device:TPU:1, one launch (start us, length us, event | category | flops | bytes accessed | tf_op | source)
XLA Modules:
  0.0 65.8 jit_solution(8280005989051420502)
XLA Ops:
  0.7 1.1 %shard_map.113 = (bf16[4,64,384]{2,1,0:T(8,128)(2,1)S(1)}, bf16[3,2,64,384]{3,2,1,0:T(8,128)(2,1)S(1)}) custom-call(bf16[2,2,64,384]{3,2,1,0:T(8,128)(2,1)} %latents_ref.1, bf16[2,2,64,384]{3,2,1,0:T(8,128)(2,1)} %cache_ref.1), custom_call_target="tpu_custom_call" | custom-call | bytes 491520 | tf_op jit(solution)/shard_map/pallas_call | solution.py:505
  1.8 4.5 %collective-permute-start = (bf16[4,64,384]{2,1,0:T(8,128)(2,1)S(1)}, bf16[4,64,384]{2,1,0:T(8,128)(2,1)S(1)}, u32[]{:S(2)}, u32[]{:S(2)}) collective-permute-start(bf16[4,64,384]{2,1,0:T(8,128)(2,1)S(1)} %get-tuple-element.28), channel_id=1, source_target_pairs={{1,2},{3,4},{5,6},{7,8},{9,10},{11,12},{13,14},{2,1},{4,3},{6,5},{... | collective-permute-start | bytes 589832 | tf_op jit(solution)/shard_map/ppermute | solution.py:517
  6.3 0.1 collective-permute-start.1
  6.4 2.7 %shard_map.114 = (bf16[3,128,384]{2,1,0:T(8,128)(2,1)S(1)}, bf16[2,3,384,1152]{3,2,1,0:T(8,128)(2,1)S(1)}) custom-call(bf16[2,128,384]{2,1,0:T(8,128)(2,1)} %bitcast.8, bf16[2,128,384]{2,1,0:T(8,128)(2,1)} %bitcast.10, bf16[3,3,3,384,384]{4,3,2,1,0:T(8,128)(2,1)} %weight_ref.3), custom_call_target="tpu_custom_call" | custom-call | bytes 10616832 | tf_op jit(solution)/shard_map/pallas_call | solution.py:525
  9.1 1.9 %collective-permute-done.edge_ref = bf16[4,64,384]{2,1,0:T(8,128)(2,1)S(1)} collective-permute-done((bf16[4,64,384]{2,1,0:T(8,128)(2,1)S(1)}, bf16[4,64,384]{2,1,0:T(8,128)(2,1)S(1)}, u32[]{:S(2)}, u32[]{:S(2)}) %collective-permute-start) | collective-permute-done | bytes 196640 | tf_op jit(solution)/shard_map/ppermute | solution.py:517
  11.1 1.4 %collective-permute-done.2.far_ref = bf16[4,64,384]{2,1,0:T(8,128)(2,1)S(1)} collective-permute-done((bf16[4,64,384]{2,1,0:T(8,128)(2,1)S(1)}, bf16[4,64,384]{2,1,0:T(8,128)(2,1)S(1)}, u32[]{:S(2)}, u32[]{:S(2)}) %collective-permute-start.2) | collective-permute-done | bytes 196640 | tf_op jit(solution)/shard_map/ppermute | solution.py:539
  12.5 4.8 %shard_map.115 = (bf16[144,384]{1,0:T(8,128)(2,1)S(1)}, bf16[144,384]{1,0:T(8,128)(2,1)S(1)}, f32[256,384]{1,0:T(8,128)S(1)}) custom-call(bf16[3,128,384]{2,1,0:T(8,128)(2,1)S(1)} %get-tuple-element.30.own_ref, bf16[3,128,384]{2,1,0:T(8,128)(2,1)S(1)} %bitcast.6, bf16[4,64,384]{2,1,0:T(8,128)(2,1)S(1)} %collective-permute-done.edge_ref, ...), custom_call_target="tpu_custom_call" | custom-call | flops 2038431744 | bytes 7962624 | tf_op jit(solution)/shard_map/pallas_call | solution.py:542
  17.3 2.3 %collective-permute-start.6 = (bf16[144,384]{1,0:T(8,128)(2,1)S(1)}, bf16[144,384]{1,0:T(8,128)(2,1)S(1)}, u32[]{:S(2)}, u32[]{:S(2)}) collective-permute-start(bf16[144,384]{1,0:T(8,128)(2,1)S(1)} %get-tuple-element.35.refs_1_.refs_11_), channel_id=1, source_target_pairs={{0,2},{1,3},{2,0},{3,1},{4,6},{5,7},{6,4},{7,5},{8,10},{9,11},{10,... | collective-permute-start | bytes 331784 | tf_op jit(solution)/shard_map/ppermute | solution.py:429
  19.6 1.3 %collective-permute-start.5 = (bf16[144,384]{1,0:T(8,128)(2,1)S(1)}, bf16[144,384]{1,0:T(8,128)(2,1)S(1)}, u32[]{:S(2)}, u32[]{:S(2)}) collective-permute-start(bf16[144,384]{1,0:T(8,128)(2,1)S(1)} %get-tuple-element.35.refs_1_.refs_11_), channel_id=1, source_target_pairs={{0,4},{1,5},{2,6},{3,7},{4,12},{5,13},{6,14},{7,15},{8,0},{9,1},{1... | collective-permute-start | bytes 331784 | tf_op jit(solution)/shard_map/ppermute | solution.py:429
  20.9 1.1 %collective-permute-start.7 = (bf16[144,384]{1,0:T(8,128)(2,1)S(1)}, bf16[144,384]{1,0:T(8,128)(2,1)S(1)}, u32[]{:S(2)}, u32[]{:S(2)}) collective-permute-start(bf16[144,384]{1,0:T(8,128)(2,1)S(1)} %get-tuple-element.34.refs_0_.refs_10_), channel_id=1, source_target_pairs={{0,8},{1,9},{2,10},{3,11},{4,0},{5,1},{6,2},{7,3},{8,12},{9,13},{1... | collective-permute-start | bytes 331784 | tf_op jit(solution)/shard_map/ppermute | solution.py:429
  22.0 0.1 collective-permute-start.4
  22.1 1.2 %collective-permute-start.3 = (bf16[144,384]{1,0:T(8,128)(2,1)S(1)}, bf16[144,384]{1,0:T(8,128)(2,1)S(1)}, u32[]{:S(2)}, u32[]{:S(2)}) collective-permute-start(bf16[144,384]{1,0:T(8,128)(2,1)S(1)} %get-tuple-element.34.refs_0_.refs_10_), channel_id=1, source_target_pairs={{0,4},{1,5},{2,6},{3,7},{4,12},{5,13},{6,14},{7,15},{8,0},{9,1},{1... | collective-permute-start | bytes 331784 | tf_op jit(solution)/shard_map/ppermute | solution.py:429
  23.2 1.3 %collective-permute-done.5.refs_3_.refs_13_ = bf16[144,384]{1,0:T(8,128)(2,1)S(1)} collective-permute-done((bf16[144,384]{1,0:T(8,128)(2,1)S(1)}, bf16[144,384]{1,0:T(8,128)(2,1)S(1)}, u32[]{:S(2)}, u32[]{:S(2)}) %collective-permute-start.5) | collective-permute-done | bytes 110624 | tf_op jit(solution)/shard_map/ppermute | solution.py:429
  24.5 5.5 %collective-permute-done.7.refs_6_.refs_16_ = bf16[144,384]{1,0:T(8,128)(2,1)S(1)} collective-permute-done((bf16[144,384]{1,0:T(8,128)(2,1)S(1)}, bf16[144,384]{1,0:T(8,128)(2,1)S(1)}, u32[]{:S(2)}, u32[]{:S(2)}) %collective-permute-start.7) | collective-permute-done | bytes 110624 | tf_op jit(solution)/shard_map/ppermute | solution.py:429
  30.0 2.4 %collective-permute-start.10 = (bf16[144,384]{1,0:T(8,128)(2,1)S(1)}, bf16[144,384]{1,0:T(8,128)(2,1)S(1)}, u32[]{:S(2)}, u32[]{:S(2)}) collective-permute-start(bf16[144,384]{1,0:T(8,128)(2,1)S(1)} %get-tuple-element.35.refs_1_.refs_11_), channel_id=1, source_target_pairs={{0,8},{1,9},{2,10},{3,11},{4,0},{5,1},{6,2},{7,3},{8,12},{9,13},{1... | collective-permute-start | bytes 331784 | tf_op jit(solution)/shard_map/ppermute | solution.py:429
  32.4 1.4 %collective-permute-start.8 = (bf16[144,384]{1,0:T(8,128)(2,1)S(1)}, bf16[144,384]{1,0:T(8,128)(2,1)S(1)}, u32[]{:S(2)}, u32[]{:S(2)}) collective-permute-start(bf16[144,384]{1,0:T(8,128)(2,1)S(1)} %collective-permute-done.3.refs_2_.refs_12_), channel_id=1, source_target_pairs={{0,4},{1,5},{2,6},{3,7},{4,12},{5,13},{6,14},{7,15},{8,0},{9,1},{1... | collective-permute-start | bytes 331784 | tf_op jit(solution)/shard_map/ppermute | solution.py:429
  33.8 5.5 %collective-permute-done.11.refs_5_.refs_15_ = bf16[144,384]{1,0:T(8,128)(2,1)S(1)} collective-permute-done((bf16[144,384]{1,0:T(8,128)(2,1)S(1)}, bf16[144,384]{1,0:T(8,128)(2,1)S(1)}, u32[]{:S(2)}, u32[]{:S(2)}) %collective-permute-start.11) | collective-permute-done | bytes 110624 | tf_op jit(solution)/shard_map/ppermute | solution.py:429
  39.4 5.4 %collective-permute-done.8.refs_4_.refs_14_ = bf16[144,384]{1,0:T(8,128)(2,1)S(1)} collective-permute-done((bf16[144,384]{1,0:T(8,128)(2,1)S(1)}, bf16[144,384]{1,0:T(8,128)(2,1)S(1)}, u32[]{:S(2)}, u32[]{:S(2)}) %collective-permute-start.8) | collective-permute-done | bytes 110624 | tf_op jit(solution)/shard_map/ppermute | solution.py:429
  44.8 1.5 %collective-permute-start.14 = (bf16[144,384]{1,0:T(8,128)(2,1)S(1)}, bf16[144,384]{1,0:T(8,128)(2,1)S(1)}, u32[]{:S(2)}, u32[]{:S(2)}) collective-permute-start(bf16[144,384]{1,0:T(8,128)(2,1)S(1)} %collective-permute-done.8.refs_4_.refs_14_), channel_id=1, source_target_pairs={{0,2},{1,3},{2,0},{3,1},{4,6},{5,7},{6,4},{7,5},{8,10},{9,11},{10,... | collective-permute-start | bytes 331784 | tf_op jit(solution)/shard_map/ppermute | solution.py:429
  46.2 4.2 %shard_map.116 = (bf16[256,384]{1,0:T(8,128)(2,1)S(1)}, f32[256,128]{1,0:T(8,128)S(1)}, f32[256,128]{1,0:T(8,128)S(1)}, f32[256,384]{1,0:T(8,128)S(1)}) custom-call(bf16[384,384]{1,0:T(8,128)(2,1)S(1)} %copy-done, bf16[384,384]{1,0:T(8,128)(2,1)S(1)} %copy-done.1, bf16[144,384]{1,0:T(8,128)(2,1)S(1)} %get-tuple-element.34.refs_0_.refs_10_, ...), custom_call_target="tpu_custom_call" | custom-call | flops 603979776 | bytes 1179648 | tf_op jit(solution)/shard_map/pallas_call | solution.py:606
  50.5 7.1 %shard_map.117 = (bf16[256,384]{1,0:T(8,128)(2,1)S(1)}, bf16[256,384]{1,0:T(8,128)(2,1)S(1)}) custom-call(bf16[256,384]{1,0:T(8,128)(2,1)S(1)} %get-tuple-element.46.refs_0_, f32[256,128]{1,0:T(8,128)S(1)} %get-tuple-element.47.refs_1_, f32[256,128]{1,0:T(8,128)S(1)} %get-tuple-element.48.refs_2_, f32[256,384]{1,0:T(8,128)S(1)} %get-tuple-element.49.refs_3_, ...), custom_call_target="tpu_custom_call" | custom-call | flops 603979776 | bytes 1572864 | tf_op jit(solution)/shard_map/pallas_call | solution.py:628
  57.6 2.7 %collective-permute-start.17 = (bf16[256,384]{1,0:T(8,128)(2,1)S(1)}, bf16[256,384]{1,0:T(8,128)(2,1)S(1)}, u32[]{:S(2)}, u32[]{:S(2)}) collective-permute-start(bf16[256,384]{1,0:T(8,128)(2,1)S(1)} %get-tuple-element.53), channel_id=1, source_target_pairs={{0,1},{1,0},{2,3},{3,2},{4,5},{5,4},{6,7},{7,6},{8,9},{9,8},{10,11... | collective-permute-start | bytes 589832 | tf_op jit(solution)/shard_map/ppermute | solution.py:668
  60.2 1.9 %shard_map.119 = bf16[2,128,384]{2,1,0:T(8,128)(2,1)} custom-call(bf16[2,128,384]{2,1,0:T(8,128)(2,1)} %bitcast.9, f32[384]{0:T(512)} %gain_ref.1), custom_call_target="tpu_custom_call" | custom-call | flops 1966080 | bytes 393216 | tf_op jit(solution)/shard_map/pallas_call | solution.py:586
  62.1 3.7 %shard_map.118 = bf16[2,4,192,128]{3,2,1,0:T(8,128)(2,1)} custom-call(bf16[256,384]{1,0:T(8,128)(2,1)S(1)} %get-tuple-element.52.mid_ref, bf16[256,384]{1,0:T(8,128)(2,1)S(1)} %collective-permute-done.17.swap_ref, bf16[3,3,192,384]{3,2,1,0:T(8,128)(2,1)S(1)} %bitcast.7), custom_call_target="tpu_custom_call" | custom-call | flops 1358954496 | bytes 1327104 | tf_op jit(solution)/shard_map/pallas_call | solution.py:671
  (33 shorter events, 0.1 us)
Async XLA Ops:
  0.6 11.9 %copy-start.5 = (f32[384]{0:T(512)S(1)}, f32[384]{0:T(512)}, u32[]{:S(2)}) copy-start(f32[384]{0:T(512)} %gain_ref.1) | copy-start | bytes 4612
  1.8 9.2 %collective-permute-start = (bf16[4,64,384]{2,1,0:T(8,128)(2,1)S(1)}, bf16[4,64,384]{2,1,0:T(8,128)(2,1)S(1)}, u32[]{:S(2)}, u32[]{:S(2)}) collective-permute-start(bf16[4,64,384]{2,1,0:T(8,128)(2,1)S(1)} %get-tuple-element.28), channel_id=1, source_target_pairs={{1,2},{3,4},{5,6},{7,8},{9,10},{11,12},{13,14},{2,1},{4,3},{6,5},{... | collective-permute-start | bytes 589832 | tf_op jit(solution)/shard_map/ppermute | solution.py:517
  6.3 4.7 %collective-permute-start.1 = (bf16[3,2,64,384]{3,2,1,0:T(8,128)(2,1)S(1)}, bf16[3,2,64,384]{3,2,1,0:T(8,128)(2,1)S(1)}, u32[]{:S(2)}, u32[]{:S(2)}) collective-permute-start(bf16[3,2,64,384]{3,2,1,0:T(8,128)(2,1)S(1)} %get-tuple-element.31), channel_id=1, source_target_pairs={{0,1},{1,0},{2,3},{3,2},{4,5},{5,4},{6,7},{7,6},{8,9},{9,8},{10,11... | collective-permute-start | bytes 884744 | tf_op jit(solution)/shard_map/ppermute | solution.py:518
  11.0 1.4 %collective-permute-start.2 = (bf16[4,64,384]{2,1,0:T(8,128)(2,1)S(1)}, bf16[4,64,384]{2,1,0:T(8,128)(2,1)S(1)}, u32[]{:S(2)}, u32[]{:S(2)}) collective-permute-start(bf16[4,64,384]{2,1,0:T(8,128)(2,1)S(1)} %collective-permute-done.edge_ref), channel_id=1, source_target_pairs={{0,1},{1,0},{2,3},{3,2},{4,5},{5,4},{6,7},{7,6},{8,9},{9,8},{10,11... | collective-permute-start | bytes 589832 | tf_op jit(solution)/shard_map/ppermute | solution.py:539
  12.5 33.7 %copy-start = (bf16[384,384]{1,0:T(8,128)(2,1)S(1)}, bf16[384,384]{1,0:T(8,128)(2,1)}, u32[]{:S(2)}) copy-start(bf16[384,384]{1,0:T(8,128)(2,1)} %refs_6_.1) | copy-start | bytes 884740
  12.5 33.7 %copy-start.1 = (bf16[384,384]{1,0:T(8,128)(2,1)S(1)}, bf16[384,384]{1,0:T(8,128)(2,1)}, u32[]{:S(2)}) copy-start(bf16[384,384]{1,0:T(8,128)(2,1)} %refs_7_.1) | copy-start | bytes 884740
  12.5 37.9 %copy-start.2 = (bf16[384,384]{1,0:T(8,128)(2,1)S(1)}, bf16[384,384]{1,0:T(8,128)(2,1)}, u32[]{:S(2)}) copy-start(bf16[384,384]{1,0:T(8,128)(2,1)} %refs_8_.1) | copy-start | bytes 884740
  12.5 37.9 %copy-start.3 = (bf16[384,384]{1,0:T(8,128)(2,1)S(1)}, bf16[384,384]{1,0:T(8,128)(2,1)}, u32[]{:S(2)}) copy-start(bf16[384,384]{1,0:T(8,128)(2,1)} %refs_9_.1) | copy-start | bytes 884740
  17.3 44.8 %copy-start.6 = (bf16[3,3,384,192]{2,3,1,0:T(8,128)(2,1)S(1)}, bf16[3,3,384,192]{2,3,1,0:T(8,128)(2,1)}, u32[]{:S(2)}) copy-start(bf16[3,3,384,192]{2,3,1,0:T(8,128)(2,1)} %param.19) | copy-start | bytes 3981316
  17.3 5.9 %collective-permute-start.6 = (bf16[144,384]{1,0:T(8,128)(2,1)S(1)}, bf16[144,384]{1,0:T(8,128)(2,1)S(1)}, u32[]{:S(2)}, u32[]{:S(2)}) collective-permute-start(bf16[144,384]{1,0:T(8,128)(2,1)S(1)} %get-tuple-element.35.refs_1_.refs_11_), channel_id=1, source_target_pairs={{0,2},{1,3},{2,0},{3,1},{4,6},{5,7},{6,4},{7,5},{8,10},{9,11},{10,... | collective-permute-start | bytes 331784 | tf_op jit(solution)/shard_map/ppermute | solution.py:429
  19.6 4.9 %collective-permute-start.5 = (bf16[144,384]{1,0:T(8,128)(2,1)S(1)}, bf16[144,384]{1,0:T(8,128)(2,1)S(1)}, u32[]{:S(2)}, u32[]{:S(2)}) collective-permute-start(bf16[144,384]{1,0:T(8,128)(2,1)S(1)} %get-tuple-element.35.refs_1_.refs_11_), channel_id=1, source_target_pairs={{0,4},{1,5},{2,6},{3,7},{4,12},{5,13},{6,14},{7,15},{8,0},{9,1},{1... | collective-permute-start | bytes 331784 | tf_op jit(solution)/shard_map/ppermute | solution.py:429
  20.9 9.0 %collective-permute-start.7 = (bf16[144,384]{1,0:T(8,128)(2,1)S(1)}, bf16[144,384]{1,0:T(8,128)(2,1)S(1)}, u32[]{:S(2)}, u32[]{:S(2)}) collective-permute-start(bf16[144,384]{1,0:T(8,128)(2,1)S(1)} %get-tuple-element.34.refs_0_.refs_10_), channel_id=1, source_target_pairs={{0,8},{1,9},{2,10},{3,11},{4,0},{5,1},{6,2},{7,3},{8,12},{9,13},{1... | collective-permute-start | bytes 331784 | tf_op jit(solution)/shard_map/ppermute | solution.py:429
  22.0 10.3 %collective-permute-start.4 = (bf16[144,384]{1,0:T(8,128)(2,1)S(1)}, bf16[144,384]{1,0:T(8,128)(2,1)S(1)}, u32[]{:S(2)}, u32[]{:S(2)}) collective-permute-start(bf16[144,384]{1,0:T(8,128)(2,1)S(1)} %get-tuple-element.34.refs_0_.refs_10_), channel_id=1, source_target_pairs={{0,2},{1,3},{2,0},{3,1},{4,6},{5,7},{6,4},{7,5},{8,10},{9,11},{10,... | collective-permute-start | bytes 331784 | tf_op jit(solution)/shard_map/ppermute | solution.py:429
  22.1 10.3 %collective-permute-start.3 = (bf16[144,384]{1,0:T(8,128)(2,1)S(1)}, bf16[144,384]{1,0:T(8,128)(2,1)S(1)}, u32[]{:S(2)}, u32[]{:S(2)}) collective-permute-start(bf16[144,384]{1,0:T(8,128)(2,1)S(1)} %get-tuple-element.34.refs_0_.refs_10_), channel_id=1, source_target_pairs={{0,4},{1,5},{2,6},{3,7},{4,12},{5,13},{6,14},{7,15},{8,0},{9,1},{1... | collective-permute-start | bytes 331784 | tf_op jit(solution)/shard_map/ppermute | solution.py:429
  30.0 9.4 %collective-permute-start.11 = (bf16[144,384]{1,0:T(8,128)(2,1)S(1)}, bf16[144,384]{1,0:T(8,128)(2,1)S(1)}, u32[]{:S(2)}, u32[]{:S(2)}) collective-permute-start(bf16[144,384]{1,0:T(8,128)(2,1)S(1)} %collective-permute-done.5.refs_3_.refs_13_), channel_id=1, source_target_pairs={{0,4},{1,5},{2,6},{3,7},{4,12},{5,13},{6,14},{7,15},{8,0},{9,1},{1... | collective-permute-start | bytes 331784 | tf_op jit(solution)/shard_map/ppermute | solution.py:429
  30.0 9.4 %collective-permute-start.10 = (bf16[144,384]{1,0:T(8,128)(2,1)S(1)}, bf16[144,384]{1,0:T(8,128)(2,1)S(1)}, u32[]{:S(2)}, u32[]{:S(2)}) collective-permute-start(bf16[144,384]{1,0:T(8,128)(2,1)S(1)} %get-tuple-element.35.refs_1_.refs_11_), channel_id=1, source_target_pairs={{0,8},{1,9},{2,10},{3,11},{4,0},{5,1},{6,2},{7,3},{8,12},{9,13},{1... | collective-permute-start | bytes 331784 | tf_op jit(solution)/shard_map/ppermute | solution.py:429
  32.3 7.0 %collective-permute-start.12 = (bf16[144,384]{1,0:T(8,128)(2,1)S(1)}, bf16[144,384]{1,0:T(8,128)(2,1)S(1)}, u32[]{:S(2)}, u32[]{:S(2)}) collective-permute-start(bf16[144,384]{1,0:T(8,128)(2,1)S(1)} %collective-permute-done.5.refs_3_.refs_13_), channel_id=1, source_target_pairs={{0,2},{1,3},{2,0},{3,1},{4,6},{5,7},{6,4},{7,5},{8,10},{9,11},{10,... | collective-permute-start | bytes 331784 | tf_op jit(solution)/shard_map/ppermute | solution.py:429
  32.3 7.0 %collective-permute-start.13 = (bf16[144,384]{1,0:T(8,128)(2,1)S(1)}, bf16[144,384]{1,0:T(8,128)(2,1)S(1)}, u32[]{:S(2)}, u32[]{:S(2)}) collective-permute-start(bf16[144,384]{1,0:T(8,128)(2,1)S(1)} %collective-permute-done.4.refs_8_.refs_18_), channel_id=1, source_target_pairs={{0,8},{1,9},{2,10},{3,11},{4,0},{5,1},{6,2},{7,3},{8,12},{9,13},{1... | collective-permute-start | bytes 331784 | tf_op jit(solution)/shard_map/ppermute | solution.py:429
  32.4 12.4 %collective-permute-start.8 = (bf16[144,384]{1,0:T(8,128)(2,1)S(1)}, bf16[144,384]{1,0:T(8,128)(2,1)S(1)}, u32[]{:S(2)}, u32[]{:S(2)}) collective-permute-start(bf16[144,384]{1,0:T(8,128)(2,1)S(1)} %collective-permute-done.3.refs_2_.refs_12_), channel_id=1, source_target_pairs={{0,4},{1,5},{2,6},{3,7},{4,12},{5,13},{6,14},{7,15},{8,0},{9,1},{1... | collective-permute-start | bytes 331784 | tf_op jit(solution)/shard_map/ppermute | solution.py:429
  39.3 5.5 %collective-permute-start.9 = (bf16[144,384]{1,0:T(8,128)(2,1)S(1)}, bf16[144,384]{1,0:T(8,128)(2,1)S(1)}, u32[]{:S(2)}, u32[]{:S(2)}) collective-permute-start(bf16[144,384]{1,0:T(8,128)(2,1)S(1)} %collective-permute-done.3.refs_2_.refs_12_), channel_id=1, source_target_pairs={{0,2},{1,3},{2,0},{3,1},{4,6},{5,7},{6,4},{7,5},{8,10},{9,11},{10,... | collective-permute-start | bytes 331784 | tf_op jit(solution)/shard_map/ppermute | solution.py:429
  39.3 11.1 %collective-permute-start.16 = (bf16[144,384]{1,0:T(8,128)(2,1)S(1)}, bf16[144,384]{1,0:T(8,128)(2,1)S(1)}, u32[]{:S(2)}, u32[]{:S(2)}) collective-permute-start(bf16[144,384]{1,0:T(8,128)(2,1)S(1)} %collective-permute-done.6.refs_9_.refs_19_), channel_id=1, source_target_pairs={{0,8},{1,9},{2,10},{3,11},{4,0},{5,1},{6,2},{7,3},{8,12},{9,13},{1... | collective-permute-start | bytes 331784 | tf_op jit(solution)/shard_map/ppermute | solution.py:429
  44.8 5.7 %collective-permute-start.15 = (bf16[144,384]{1,0:T(8,128)(2,1)S(1)}, bf16[144,384]{1,0:T(8,128)(2,1)S(1)}, u32[]{:S(2)}, u32[]{:S(2)}) collective-permute-start(bf16[144,384]{1,0:T(8,128)(2,1)S(1)} %collective-permute-done.11.refs_5_.refs_15_), channel_id=1, source_target_pairs={{0,2},{1,3},{2,0},{3,1},{4,6},{5,7},{6,4},{7,5},{8,10},{9,11},{10,... | collective-permute-start | bytes 331784 | tf_op jit(solution)/shard_map/ppermute | solution.py:429
  44.8 5.7 %collective-permute-start.14 = (bf16[144,384]{1,0:T(8,128)(2,1)S(1)}, bf16[144,384]{1,0:T(8,128)(2,1)S(1)}, u32[]{:S(2)}, u32[]{:S(2)}) collective-permute-start(bf16[144,384]{1,0:T(8,128)(2,1)S(1)} %collective-permute-done.8.refs_4_.refs_14_), channel_id=1, source_target_pairs={{0,2},{1,3},{2,0},{3,1},{4,6},{5,7},{6,4},{7,5},{8,10},{9,11},{10,... | collective-permute-start | bytes 331784 | tf_op jit(solution)/shard_map/ppermute | solution.py:429
  57.6 4.6 %collective-permute-start.17 = (bf16[256,384]{1,0:T(8,128)(2,1)S(1)}, bf16[256,384]{1,0:T(8,128)(2,1)S(1)}, u32[]{:S(2)}, u32[]{:S(2)}) collective-permute-start(bf16[256,384]{1,0:T(8,128)(2,1)S(1)} %get-tuple-element.53), channel_id=1, source_target_pairs={{0,1},{1,0},{2,3},{3,2},{4,5},{5,4},{6,7},{7,6},{8,9},{9,8},{10,11... | collective-permute-start | bytes 589832 | tf_op jit(solution)/shard_map/ppermute | solution.py:668
  (1 other events, 11.9 us)
